TPU v7x, 256 devices: a whole 4x4x8 slice. The times are simulated.
256 devices in a mesh: gx: 16 (over x, y_lo, core), ha: 16 (over z, y_hi).
Axes of the slice: x: 4, y: 4 (y_hi: 2, y_lo: 2; y = y_hi * 2 + y_lo), z: 8, core: 2. Of those that a mesh axis runs over, the one named last changes fastest.
Arguments:
- value_field: float32 [4, 64, 128, 128], P(None, 'gx', 'ha'), may hold values from -6 to 6
- wind_grid: int32 [2, 2, 64, 128], P(None, None, 'gx'), may hold values from -1023 to 1023
- obstacle: int32 [64, 128], P('gx'), may hold values 0 or 1
Outputs:
- value_next: float32 [4, 64, 128, 128], P(None, 'gx', 'ha')
All inputs are finite; a program needn't handle non-finite values. Where the computation divides by a largest or mean magnitude, that divisor is 1e-20 or more. No bound on the sum of `obstacle` on one device may be relied on, other than what follows from the above.
Results may differ from a plain program's by a relative error of at most 0.0003.
Values sent between devices are 32-bit elements; how exact they have to be, the bound alone decides.
A program may use at most 64 MiB of HBM per device.

v0:
```python
import math

import jax
import jax.numpy as jnp
from jax import lax
from jax.sharding import PartitionSpec as P

NH = 128
STEPS = 2


TURN_RATE = 0.25
ACCEL_MAX = 0.5
SPEED_BASE = 0.5
SPEED_STEP = 0.25
SPEED_MAX = 1.25
WIND_SCALE = 1.0 / 512.0
CFL_NUMBER = 0.8
OBSTACLE_LEVEL = 1.0


def with_halo(block, sides, width, periodic):
    for axis, dim in sides:
        count = lax.axis_size(axis)
        forward = [(i, i + 1) for i in range(count - 1)]
        if periodic:
            forward.append((count - 1, 0))
        backward = [(target, source) for source, target in forward]
        low = lax.ppermute(
            lax.slice_in_dim(block, block.shape[dim] - width, None, axis=dim), axis, forward
        )
        high = lax.ppermute(lax.slice_in_dim(block, 0, width, axis=dim), axis, backward)
        block = jnp.concatenate([low, block, high], axis=dim)
    return block


def minmod(left_term, right_term):
    return (
        0.5
        * (jnp.sign(left_term) + jnp.sign(right_term))
        * jnp.minimum(jnp.abs(left_term), jnp.abs(right_term))
    )


def part_of(source, begin, finish, dimension):
    return lax.slice_in_dim(source, begin, finish, axis=dimension)


def slopes(padded, dimension, spacing):
    padded_extent = padded.shape[dimension]
    inner_count = padded_extent - 4
    first_diff = part_of(padded, 1, padded_extent, dimension) - part_of(
        padded, 0, padded_extent - 1, dimension
    )
    second_diff = part_of(first_diff, 1, inner_count + 3, dimension) - part_of(
        first_diff, 0, inner_count + 2, dimension
    )
    limited = minmod(
        part_of(second_diff, 0, inner_count + 1, dimension),
        part_of(second_diff, 1, inner_count + 2, dimension),
    )
    backward = (
        part_of(first_diff, 1, inner_count + 1, dimension)
        + 0.5 * part_of(limited, 0, inner_count, dimension)
    ) / spacing
    forward = (
        part_of(first_diff, 2, inner_count + 2, dimension)
        - 0.5 * part_of(limited, 1, inner_count + 1, dimension)
    ) / spacing
    return (0.5 * (backward + forward), forward - backward)


def extend(source, dimension):
    extent = source.shape[dimension]
    first_plane = part_of(source, 0, 1, dimension)
    second_plane = part_of(source, 1, 2, dimension)
    last_plane = part_of(source, extent - 1, extent, dimension)
    before_plane = part_of(source, extent - 2, extent - 1, dimension)
    return jnp.concatenate(
        [
            3.0 * first_plane - 2.0 * second_plane,
            2.0 * first_plane - second_plane,
            source,
            2.0 * last_plane - before_plane,
            3.0 * last_plane - 2.0 * before_plane,
        ],
        axis=dimension,
    )


def rate(
    center, along_x, along_head, wind_x, wind_y, head_cos, head_sin, alpha_x, alpha_y, head_step
):
    mean_x, jump_x = slopes(along_x, 1, 1.0)
    mean_h, jump_h = slopes(along_head, 2, head_step)
    mean_y, jump_y = slopes(extend(center, 3), 3, 1.0)
    mean_s, jump_s = slopes(extend(center, 0), 0, SPEED_STEP)
    speeds = (SPEED_BASE + SPEED_STEP * jnp.arange(center.shape[0], dtype=jnp.float32))[
        :, None, None, None
    ]
    velocity_x = speeds * head_cos[None, None, :, None] + wind_x[None, :, None, :]
    velocity_y = speeds * head_sin[None, None, :, None] + wind_y[None, :, None, :]
    hamilton = (
        mean_x * velocity_x
        + mean_y * velocity_y
        - TURN_RATE * jnp.abs(mean_h)
        - ACCEL_MAX * jnp.abs(mean_s)
    )
    return hamilton + 0.5 * (
        alpha_x * jump_x + alpha_y * jump_y + TURN_RATE * jump_h + ACCEL_MAX * jump_s
    )


def time_step(alpha_x, alpha_y, head_step):
    return CFL_NUMBER / (alpha_x + alpha_y + TURN_RATE / head_step + ACCEL_MAX / SPEED_STEP)


def fix_ends(padded, width):
    device_count = lax.axis_size("gx")
    device_place = lax.axis_index("gx")
    padded_extent = padded.shape[1]
    first_plane = padded[:, width : width + 1]
    second_plane = padded[:, width + 1 : width + 2]
    last_plane = padded[:, padded_extent - width - 1 : padded_extent - width]
    before_plane = padded[:, padded_extent - width - 2 : padded_extent - width - 1]
    lower_rim = padded[:, :width]
    upper_rim = padded[:, padded_extent - width :]
    fixed_lower = jnp.concatenate(
        [
            lower_rim[:, : width - 2],
            3.0 * first_plane - 2.0 * second_plane,
            2.0 * first_plane - second_plane,
        ],
        axis=1,
    )
    fixed_upper = jnp.concatenate(
        [2.0 * last_plane - before_plane, 3.0 * last_plane - 2.0 * before_plane, upper_rim[:, 2:]],
        axis=1,
    )
    lower_rim = jnp.where(device_place == 0, fixed_lower, lower_rim)
    upper_rim = jnp.where(device_place == device_count - 1, fixed_upper, upper_rim)
    return jnp.concatenate([lower_rim, padded[:, width : padded_extent - width], upper_rim], axis=1)


def head_angles(margin, extent, heads_dev, head_step):
    head_index = jnp.mod(
        lax.axis_index("ha") * heads_dev - margin + jnp.arange(extent, dtype=jnp.int32), NH
    )
    angles = head_index.astype(jnp.float32) * head_step
    return (jnp.cos(angles), jnp.sin(angles))


def local_rate(field, wind_x, wind_y, head_cos, head_sin, alpha_x, alpha_y, head_step):
    along_x = fix_ends(with_halo(field, (("gx", 1),), 2, False), 2)
    along_head = with_halo(field, (("ha", 2),), 2, True)
    return rate(
        field, along_x, along_head, wind_x, wind_y, head_cos, head_sin, alpha_x, alpha_y, head_step
    )


def local(value_field, wind_grid, obstacle):
    head_step = 2.0 * math.pi / NH
    heads_dev = value_field.shape[2]
    winds = wind_grid.astype(jnp.float32) * WIND_SCALE
    blocked = (obstacle == 1)[None, :, None, :]
    head_cos, head_sin = head_angles(0, heads_dev, heads_dev, head_step)
    field = value_field
    for step_index in range(STEPS):
        wind_x = winds[step_index, 0]
        wind_y = winds[step_index, 1]
        peaks = lax.pmax(jnp.max(jnp.abs(winds[step_index]), axis=(1, 2)), "gx")
        alpha_x = SPEED_MAX + peaks[0]
        alpha_y = SPEED_MAX + peaks[1]
        delta_time = time_step(alpha_x, alpha_y, head_step)
        section = field + delta_time * local_rate(
            field, wind_x, wind_y, head_cos, head_sin, alpha_x, alpha_y, head_step
        )
        second_rate = local_rate(
            section, wind_x, wind_y, head_cos, head_sin, alpha_x, alpha_y, head_step
        )
        candidate = 0.5 * field + 0.5 * (section + delta_time * second_rate)
        field = jnp.where(blocked, jnp.maximum(candidate, OBSTACLE_LEVEL), candidate)
    return field


def solution(mesh):
    placed = (P(None, "gx", "ha", None), P(None, None, "gx", None), P("gx", None))
    return jax.shard_map(
        local, mesh=mesh, in_specs=placed, out_specs=P(None, "gx", "ha", None), check_vma=False
    )
```

profile of v0, /device:TPU:88, one launch (start us, length us, event | category | flops | bytes accessed | tf_op | source)
XLA Modules:
  0.0 92.1 jit_solution(9955721289758917912)
XLA Ops:
  0.0 0.8 fusion.89
  0.8 1.9 %collective-permute-start = (f32[4,2,8,128]{3,2,1,0:T(8,128)S(1)}, f32[4,2,8,128]{3,2,1,0:T(8,128)S(1)}, u32[]{:S(2)}, u32[]{:S(2)}) collective-permute-start(f32[4,2,8,128]{3,2,1,0:T(8,128)S(1)} %get-tuple-element.61), channel_id=1, source_target_pairs={{0,16},{16,32},{32,48},{48,64},{64,80},{80,96},{96,112},{112,128},... | collective-permute-start | bytes 98312 | tf_op jit(solution)/shard_map/ppermute | solution.py:29
  2.8 3.6 %collective-permute-start.1 = (f32[4,2,8,128]{3,2,1,0:T(8,128)S(1)}, f32[4,2,8,128]{3,2,1,0:T(8,128)S(1)}, u32[]{:S(2)}, u32[]{:S(2)}) collective-permute-start(f32[4,2,8,128]{3,2,1,0:T(8,128)S(1)} %get-tuple-element.62), channel_id=1, source_target_pairs={{16,0},{32,16},{48,32},{64,48},{80,64},{96,80},{112,96},{128,112},... | collective-permute-start | bytes 98312 | tf_op jit(solution)/shard_map/ppermute | solution.py:32
  6.4 2.7 %collective-permute-start.2 = (f32[4,4,2,128]{3,2,1,0:T(2,128)S(1)}, f32[4,4,2,128]{3,2,1,0:T(2,128)S(1)}, u32[]{:S(2)}, u32[]{:S(2)}) collective-permute-start(f32[4,4,2,128]{3,2,1,0:T(2,128)S(1)} %get-tuple-element.67), channel_id=1, source_target_pairs={{0,1},{1,2},{2,3},{3,4},{4,5},{5,6},{6,7},{7,8},{8,9},{9,10},{10,1... | collective-permute-start | bytes 49160 | tf_op jit(solution)/shard_map/ppermute | solution.py:29
  9.1 0.9 %collective-permute-start.3 = (f32[4,4,2,128]{3,2,1,0:T(2,128)S(1)}, f32[4,4,2,128]{3,2,1,0:T(2,128)S(1)}, u32[]{:S(2)}, u32[]{:S(2)}) collective-permute-start(f32[4,4,2,128]{3,2,1,0:T(2,128)S(1)} %get-tuple-element.68), channel_id=1, source_target_pairs={{1,0},{2,1},{3,2},{4,3},{5,4},{6,5},{7,6},{8,7},{9,8},{10,9},{11,1... | collective-permute-start | bytes 49160 | tf_op jit(solution)/shard_map/ppermute | solution.py:32
  10.1 0.1 multiply_subtract_fusion.12
  10.2 0.0 copy-start.1
  10.2 0.7 copy-done.1
  10.9 0.1 fusion.76
  11.0 0.2 maximum_subtract_fusion
  11.2 0.1 slice_subtract_fusion.11
  11.3 0.1 minimum_multiply_fusion.7
  11.5 0.0 copy-start.2
  11.6 0.1 fusion.81
  11.6 0.6 copy-done.2
  12.2 24.8 %all-reduce = (f32[2]{0:T(128)S(1)}, f32[2]{0:T(128)S(1)}) all-reduce(f32[2]{0:T(128)S(1)} %get-tuple-element.6, f32[2]{0:T(128)S(1)} %get-tuple-element.5), channel_id=1, replica_groups=mesh['gx'=16,'ha'=16] {'gx'}, use_global_device_ids=true, to_apply=%region_1.2 | all-reduce | flops 4 | bytes 32 | tf_op jit(solution)/shard_map/pmax | solution.py:171
  37.0 0.1 broadcast_multiply_fusion.1
  37.1 0.6 fusion.91
  40.4 0.0 collective-permute-done.2
  40.4 0.0 collective-permute-done.3
  40.5 0.1 minimum_multiply_fusion.6
  40.6 0.0 collective-permute-done
  40.6 0.0 collective-permute-done.1
  40.7 0.2 fusion.5
  40.9 0.1 multiply_subtract_fusion.8
  41.1 1.9 %collective-permute-start.4 = (f32[4,2,8,128]{3,2,1,0:T(8,128)S(1)}, f32[4,2,8,128]{3,2,1,0:T(8,128)S(1)}, u32[]{:S(2)}, u32[]{:S(2)}) collective-permute-start(f32[4,2,8,128]{3,2,1,0:T(8,128)S(1)} %get-tuple-element.45), channel_id=1, source_target_pairs={{0,16},{16,32},{32,48},{48,64},{64,80},{80,96},{96,112},{112,128},... | collective-permute-start | bytes 98312 | tf_op jit(solution)/shard_map/ppermute | solution.py:29
  43.0 4.2 %collective-permute-start.5 = (f32[4,2,8,128]{3,2,1,0:T(8,128)S(1)}, f32[4,2,8,128]{3,2,1,0:T(8,128)S(1)}, u32[]{:S(2)}, u32[]{:S(2)}) collective-permute-start(f32[4,2,8,128]{3,2,1,0:T(8,128)S(1)} %get-tuple-element.46), channel_id=1, source_target_pairs={{16,0},{32,16},{48,32},{64,48},{80,64},{96,80},{112,96},{128,112},... | collective-permute-start | bytes 98312 | tf_op jit(solution)/shard_map/ppermute | solution.py:32
  47.2 0.2 maximum_subtract_fusion.1
  47.4 0.1 slice_subtract_fusion.8
  47.5 0.1 minimum_multiply_fusion.5
  47.7 3.6 %collective-permute-start.6 = (f32[4,4,2,128]{3,2,1,0:T(2,128)S(1)}, f32[4,4,2,128]{3,2,1,0:T(2,128)S(1)}, u32[]{:S(2)}, u32[]{:S(2)}) collective-permute-start(f32[4,4,2,128]{3,2,1,0:T(2,128)S(1)} %get-tuple-element.51), channel_id=1, source_target_pairs={{0,1},{1,2},{2,3},{3,4},{4,5},{5,6},{6,7},{7,8},{8,9},{9,10},{10,1... | collective-permute-start | bytes 49160 | tf_op jit(solution)/shard_map/ppermute | solution.py:29
  51.2 0.0 collective-permute-start.7
  51.4 1.6 %collective-permute-done.6 = f32[4,4,2,128]{3,2,1,0:T(2,128)S(1)} collective-permute-done((f32[4,4,2,128]{3,2,1,0:T(2,128)S(1)}, f32[4,4,2,128]{3,2,1,0:T(2,128)S(1)}, u32[]{:S(2)}, u32[]{:S(2)}) %collective-permute-start.6) | collective-permute-done | bytes 16416 | tf_op jit(solution)/shard_map/ppermute | solution.py:29
  53.0 4.4 %collective-permute-done.7 = f32[4,4,2,128]{3,2,1,0:T(2,128)S(1)} collective-permute-done((f32[4,4,2,128]{3,2,1,0:T(2,128)S(1)}, f32[4,4,2,128]{3,2,1,0:T(2,128)S(1)}, u32[]{:S(2)}, u32[]{:S(2)}) %collective-permute-start.7) | collective-permute-done | bytes 16416 | tf_op jit(solution)/shard_map/ppermute | solution.py:32
  57.5 0.1 minimum_multiply_fusion.4
  57.6 0.0 collective-permute-done.4
  57.6 0.0 collective-permute-done.5
  57.7 0.2 maximum_select_fusion.1
  57.9 0.1 multiply_subtract_fusion.4
  58.1 1.9 %collective-permute-start.8 = (f32[4,2,8,128]{3,2,1,0:T(8,128)S(1)}, f32[4,2,8,128]{3,2,1,0:T(8,128)S(1)}, u32[]{:S(2)}, u32[]{:S(2)}) collective-permute-start(f32[4,2,8,128]{3,2,1,0:T(8,128)S(1)} %get-tuple-element.29), channel_id=1, source_target_pairs={{0,16},{16,32},{32,48},{48,64},{64,80},{80,96},{96,112},{112,128},... | collective-permute-start | bytes 98312 | tf_op jit(solution)/shard_map/ppermute | solution.py:29
  60.0 3.6 %collective-permute-start.9 = (f32[4,2,8,128]{3,2,1,0:T(8,128)S(1)}, f32[4,2,8,128]{3,2,1,0:T(8,128)S(1)}, u32[]{:S(2)}, u32[]{:S(2)}) collective-permute-start(f32[4,2,8,128]{3,2,1,0:T(8,128)S(1)} %get-tuple-element.30), channel_id=1, source_target_pairs={{16,0},{32,16},{48,32},{64,48},{80,64},{96,80},{112,96},{128,112},... | collective-permute-start | bytes 98312 | tf_op jit(solution)/shard_map/ppermute | solution.py:32
  63.7 0.2 maximum_subtract_fusion.2
  63.9 0.1 slice_subtract_fusion.5
  64.0 0.1 minimum_multiply_fusion.3
  64.1 3.0 %collective-permute-start.10 = (f32[4,4,2,128]{3,2,1,0:T(2,128)S(1)}, f32[4,4,2,128]{3,2,1,0:T(2,128)S(1)}, u32[]{:S(2)}, u32[]{:S(2)}) collective-permute-start(f32[4,4,2,128]{3,2,1,0:T(2,128)S(1)} %get-tuple-element.35), channel_id=1, source_target_pairs={{0,1},{1,2},{2,3},{3,4},{4,5},{5,6},{6,7},{7,8},{8,9},{9,10},{10,1... | collective-permute-start | bytes 49160 | tf_op jit(solution)/shard_map/ppermute | solution.py:29
  67.1 0.6 collective-permute-start.11
  67.8 1.6 %collective-permute-done.10 = f32[4,4,2,128]{3,2,1,0:T(2,128)S(1)} collective-permute-done((f32[4,4,2,128]{3,2,1,0:T(2,128)S(1)}, f32[4,4,2,128]{3,2,1,0:T(2,128)S(1)}, u32[]{:S(2)}, u32[]{:S(2)}) %collective-permute-start.10) | collective-permute-done | bytes 16416 | tf_op jit(solution)/shard_map/ppermute | solution.py:29
  69.4 5.0 %collective-permute-done.11 = f32[4,4,2,128]{3,2,1,0:T(2,128)S(1)} collective-permute-done((f32[4,4,2,128]{3,2,1,0:T(2,128)S(1)}, f32[4,4,2,128]{3,2,1,0:T(2,128)S(1)}, u32[]{:S(2)}, u32[]{:S(2)}) %collective-permute-start.11) | collective-permute-done | bytes 16416 | tf_op jit(solution)/shard_map/ppermute | solution.py:32
  74.5 0.1 minimum_multiply_fusion.2
  74.6 0.0 collective-permute-done.8
  74.6 0.0 collective-permute-done.9
  74.8 0.2 fusion.19
  75.0 0.1 multiply_subtract_fusion
  75.1 1.9 %collective-permute-start.12 = (f32[4,2,8,128]{3,2,1,0:T(8,128)S(1)}, f32[4,2,8,128]{3,2,1,0:T(8,128)S(1)}, u32[]{:S(2)}, u32[]{:S(2)}) collective-permute-start(f32[4,2,8,128]{3,2,1,0:T(8,128)S(1)} %get-tuple-element.13), channel_id=1, source_target_pairs={{0,16},{16,32},{32,48},{48,64},{64,80},{80,96},{96,112},{112,128},... | collective-permute-start | bytes 98312 | tf_op jit(solution)/shard_map/ppermute | solution.py:29
  77.0 3.6 %collective-permute-start.13 = (f32[4,2,8,128]{3,2,1,0:T(8,128)S(1)}, f32[4,2,8,128]{3,2,1,0:T(8,128)S(1)}, u32[]{:S(2)}, u32[]{:S(2)}) collective-permute-start(f32[4,2,8,128]{3,2,1,0:T(8,128)S(1)} %get-tuple-element.14), channel_id=1, source_target_pairs={{16,0},{32,16},{48,32},{64,48},{80,64},{96,80},{112,96},{128,112},... | collective-permute-start | bytes 98312 | tf_op jit(solution)/shard_map/ppermute | solution.py:32
  80.7 0.2 maximum_subtract_fusion.3
  80.9 0.1 slice_subtract_fusion.2
  81.0 0.1 minimum_multiply_fusion.1
  81.2 3.6 %collective-permute-start.14 = (f32[4,4,2,128]{3,2,1,0:T(2,128)S(1)}, f32[4,4,2,128]{3,2,1,0:T(2,128)S(1)}, u32[]{:S(2)}, u32[]{:S(2)}) collective-permute-start(f32[4,4,2,128]{3,2,1,0:T(2,128)S(1)} %get-tuple-element.19), channel_id=1, source_target_pairs={{0,1},{1,2},{2,3},{3,4},{4,5},{5,6},{6,7},{7,8},{8,9},{9,10},{10,1... | collective-permute-start | bytes 49160 | tf_op jit(solution)/shard_map/ppermute | solution.py:29
  84.9 1.6 %collective-permute-done.14 = f32[4,4,2,128]{3,2,1,0:T(2,128)S(1)} collective-permute-done((f32[4,4,2,128]{3,2,1,0:T(2,128)S(1)}, f32[4,4,2,128]{3,2,1,0:T(2,128)S(1)}, u32[]{:S(2)}, u32[]{:S(2)}) %collective-permute-start.14) | collective-permute-done | bytes 16416 | tf_op jit(solution)/shard_map/ppermute | solution.py:29
  86.5 4.4 %collective-permute-done.15 = f32[4,4,2,128]{3,2,1,0:T(2,128)S(1)} collective-permute-done((f32[4,4,2,128]{3,2,1,0:T(2,128)S(1)}, f32[4,4,2,128]{3,2,1,0:T(2,128)S(1)}, u32[]{:S(2)}, u32[]{:S(2)}) %collective-permute-start.15) | collective-permute-done | bytes 16416 | tf_op jit(solution)/shard_map/ppermute | solution.py:32
  91.0 0.1 minimum_multiply_fusion
  91.1 0.0 collective-permute-done.13
  91.2 0.8 maximum_select_fusion
  (71 shorter events, 1.0 us)
Async XLA Ops:
  0.0 6.4 %copy-start = (f32[4,4,8,128]{3,2,1,0:T(8,128)S(1)}, f32[4,4,8,128]{3,2,1,0:T(8,128)}, u32[]{:S(2)}) copy-start(f32[4,4,8,128]{3,2,1,0:T(8,128)} %param.3) | copy-start | bytes 196612
  0.8 39.7 %collective-permute-start = (f32[4,2,8,128]{3,2,1,0:T(8,128)S(1)}, f32[4,2,8,128]{3,2,1,0:T(8,128)S(1)}, u32[]{:S(2)}, u32[]{:S(2)}) collective-permute-start(f32[4,2,8,128]{3,2,1,0:T(8,128)S(1)} %get-tuple-element.61), channel_id=1, source_target_pairs={{0,16},{16,32},{32,48},{48,64},{64,80},{80,96},{96,112},{112,128},... | collective-permute-start | bytes 98312 | tf_op jit(solution)/shard_map/ppermute | solution.py:29
  2.8 37.8 %collective-permute-start.1 = (f32[4,2,8,128]{3,2,1,0:T(8,128)S(1)}, f32[4,2,8,128]{3,2,1,0:T(8,128)S(1)}, u32[]{:S(2)}, u32[]{:S(2)}) collective-permute-start(f32[4,2,8,128]{3,2,1,0:T(8,128)S(1)} %get-tuple-element.62), channel_id=1, source_target_pairs={{16,0},{32,16},{48,32},{64,48},{80,64},{96,80},{112,96},{128,112},... | collective-permute-start | bytes 98312 | tf_op jit(solution)/shard_map/ppermute | solution.py:32
  6.4 33.9 %collective-permute-start.2 = (f32[4,4,2,128]{3,2,1,0:T(2,128)S(1)}, f32[4,4,2,128]{3,2,1,0:T(2,128)S(1)}, u32[]{:S(2)}, u32[]{:S(2)}) collective-permute-start(f32[4,4,2,128]{3,2,1,0:T(2,128)S(1)} %get-tuple-element.67), channel_id=1, source_target_pairs={{0,1},{1,2},{2,3},{3,4},{4,5},{5,6},{6,7},{7,8},{8,9},{9,10},{10,1... | collective-permute-start | bytes 49160 | tf_op jit(solution)/shard_map/ppermute | solution.py:29
  9.1 31.3 %collective-permute-start.3 = (f32[4,4,2,128]{3,2,1,0:T(2,128)S(1)}, f32[4,4,2,128]{3,2,1,0:T(2,128)S(1)}, u32[]{:S(2)}, u32[]{:S(2)}) collective-permute-start(f32[4,4,2,128]{3,2,1,0:T(2,128)S(1)} %get-tuple-element.68), channel_id=1, source_target_pairs={{1,0},{2,1},{3,2},{4,3},{5,4},{6,5},{7,6},{8,7},{9,8},{10,9},{11,1... | collective-permute-start | bytes 49160 | tf_op jit(solution)/shard_map/ppermute | solution.py:32
  10.2 0.7 copy-start.1
  11.5 0.7 copy-start.2
  41.1 16.5 %collective-permute-start.4 = (f32[4,2,8,128]{3,2,1,0:T(8,128)S(1)}, f32[4,2,8,128]{3,2,1,0:T(8,128)S(1)}, u32[]{:S(2)}, u32[]{:S(2)}) collective-permute-start(f32[4,2,8,128]{3,2,1,0:T(8,128)S(1)} %get-tuple-element.45), channel_id=1, source_target_pairs={{0,16},{16,32},{32,48},{48,64},{64,80},{80,96},{96,112},{112,128},... | collective-permute-start | bytes 98312 | tf_op jit(solution)/shard_map/ppermute | solution.py:29
  43.0 14.6 %collective-permute-start.5 = (f32[4,2,8,128]{3,2,1,0:T(8,128)S(1)}, f32[4,2,8,128]{3,2,1,0:T(8,128)S(1)}, u32[]{:S(2)}, u32[]{:S(2)}) collective-permute-start(f32[4,2,8,128]{3,2,1,0:T(8,128)S(1)} %get-tuple-element.46), channel_id=1, source_target_pairs={{16,0},{32,16},{48,32},{64,48},{80,64},{96,80},{112,96},{128,112},... | collective-permute-start | bytes 98312 | tf_op jit(solution)/shard_map/ppermute | solution.py:32
  47.7 5.3 %collective-permute-start.6 = (f32[4,4,2,128]{3,2,1,0:T(2,128)S(1)}, f32[4,4,2,128]{3,2,1,0:T(2,128)S(1)}, u32[]{:S(2)}, u32[]{:S(2)}) collective-permute-start(f32[4,4,2,128]{3,2,1,0:T(2,128)S(1)} %get-tuple-element.51), channel_id=1, source_target_pairs={{0,1},{1,2},{2,3},{3,4},{4,5},{5,6},{6,7},{7,8},{8,9},{9,10},{10,1... | collective-permute-start | bytes 49160 | tf_op jit(solution)/shard_map/ppermute | solution.py:29
  51.2 6.1 %collective-permute-start.7 = (f32[4,4,2,128]{3,2,1,0:T(2,128)S(1)}, f32[4,4,2,128]{3,2,1,0:T(2,128)S(1)}, u32[]{:S(2)}, u32[]{:S(2)}) collective-permute-start(f32[4,4,2,128]{3,2,1,0:T(2,128)S(1)} %get-tuple-element.52), channel_id=1, source_target_pairs={{1,0},{2,1},{3,2},{4,3},{5,4},{6,5},{7,6},{8,7},{9,8},{10,9},{11,1... | collective-permute-start | bytes 49160 | tf_op jit(solution)/shard_map/ppermute | solution.py:32
  58.1 16.5 %collective-permute-start.8 = (f32[4,2,8,128]{3,2,1,0:T(8,128)S(1)}, f32[4,2,8,128]{3,2,1,0:T(8,128)S(1)}, u32[]{:S(2)}, u32[]{:S(2)}) collective-permute-start(f32[4,2,8,128]{3,2,1,0:T(8,128)S(1)} %get-tuple-element.29), channel_id=1, source_target_pairs={{0,16},{16,32},{32,48},{48,64},{64,80},{80,96},{96,112},{112,128},... | collective-permute-start | bytes 98312 | tf_op jit(solution)/shard_map/ppermute | solution.py:29
  60.0 14.6 %collective-permute-start.9 = (f32[4,2,8,128]{3,2,1,0:T(8,128)S(1)}, f32[4,2,8,128]{3,2,1,0:T(8,128)S(1)}, u32[]{:S(2)}, u32[]{:S(2)}) collective-permute-start(f32[4,2,8,128]{3,2,1,0:T(8,128)S(1)} %get-tuple-element.30), channel_id=1, source_target_pairs={{16,0},{32,16},{48,32},{64,48},{80,64},{96,80},{112,96},{128,112},... | collective-permute-start | bytes 98312 | tf_op jit(solution)/shard_map/ppermute | solution.py:32
  64.1 5.3 %collective-permute-start.10 = (f32[4,4,2,128]{3,2,1,0:T(2,128)S(1)}, f32[4,4,2,128]{3,2,1,0:T(2,128)S(1)}, u32[]{:S(2)}, u32[]{:S(2)}) collective-permute-start(f32[4,4,2,128]{3,2,1,0:T(2,128)S(1)} %get-tuple-element.35), channel_id=1, source_target_pairs={{0,1},{1,2},{2,3},{3,4},{4,5},{5,6},{6,7},{7,8},{8,9},{9,10},{10,1... | collective-permute-start | bytes 49160 | tf_op jit(solution)/shard_map/ppermute | solution.py:29
  67.1 7.4 %collective-permute-start.11 = (f32[4,4,2,128]{3,2,1,0:T(2,128)S(1)}, f32[4,4,2,128]{3,2,1,0:T(2,128)S(1)}, u32[]{:S(2)}, u32[]{:S(2)}) collective-permute-start(f32[4,4,2,128]{3,2,1,0:T(2,128)S(1)} %get-tuple-element.36), channel_id=1, source_target_pairs={{1,0},{2,1},{3,2},{4,3},{5,4},{6,5},{7,6},{8,7},{9,8},{10,9},{11,1... | collective-permute-start | bytes 49160 | tf_op jit(solution)/shard_map/ppermute | solution.py:32
  75.1 16.0 %collective-permute-start.12 = (f32[4,2,8,128]{3,2,1,0:T(8,128)S(1)}, f32[4,2,8,128]{3,2,1,0:T(8,128)S(1)}, u32[]{:S(2)}, u32[]{:S(2)}) collective-permute-start(f32[4,2,8,128]{3,2,1,0:T(8,128)S(1)} %get-tuple-element.13), channel_id=1, source_target_pairs={{0,16},{16,32},{32,48},{48,64},{64,80},{80,96},{96,112},{112,128},... | collective-permute-start | bytes 98312 | tf_op jit(solution)/shard_map/ppermute | solution.py:29
  77.0 14.1 %collective-permute-start.13 = (f32[4,2,8,128]{3,2,1,0:T(8,128)S(1)}, f32[4,2,8,128]{3,2,1,0:T(8,128)S(1)}, u32[]{:S(2)}, u32[]{:S(2)}) collective-permute-start(f32[4,2,8,128]{3,2,1,0:T(8,128)S(1)} %get-tuple-element.14), channel_id=1, source_target_pairs={{16,0},{32,16},{48,32},{64,48},{80,64},{96,80},{112,96},{128,112},... | collective-permute-start | bytes 98312 | tf_op jit(solution)/shard_map/ppermute | solution.py:32
  81.2 5.3 %collective-permute-start.14 = (f32[4,4,2,128]{3,2,1,0:T(2,128)S(1)}, f32[4,4,2,128]{3,2,1,0:T(2,128)S(1)}, u32[]{:S(2)}, u32[]{:S(2)}) collective-permute-start(f32[4,4,2,128]{3,2,1,0:T(2,128)S(1)} %get-tuple-element.19), channel_id=1, source_target_pairs={{0,1},{1,2},{2,3},{3,4},{4,5},{5,6},{6,7},{7,8},{8,9},{9,10},{10,1... | collective-permute-start | bytes 49160 | tf_op jit(solution)/shard_map/ppermute | solution.py:29
  84.8 6.1 %collective-permute-start.15 = (f32[4,4,2,128]{3,2,1,0:T(2,128)S(1)}, f32[4,4,2,128]{3,2,1,0:T(2,128)S(1)}, u32[]{:S(2)}, u32[]{:S(2)}) collective-permute-start(f32[4,4,2,128]{3,2,1,0:T(2,128)S(1)} %get-tuple-element.20), channel_id=1, source_target_pairs={{1,0},{2,1},{3,2},{4,3},{5,4},{6,5},{7,6},{8,7},{9,8},{10,9},{11,1... | collective-permute-start | bytes 49160 | tf_op jit(solution)/shard_map/ppermute | solution.py:32
where the time goes:
time: 92.5 us; the launch traced here: 92.1 us
  starting transfers between devices  37.2 us (40%)
  blocking collectives  24.8 us (27%)
  waiting for transfers between devices  18.7 us (20%)
  other arithmetic  5.15 us (6%)
  between operations  3.39 us (4%)
  local copies, waits for them, and re-layouts  2.85 us (3%)
    pmax x1, blocking collectives, local(): peaks = lax.pmax(jnp.max(jnp.abs(winds[step_index]), axis=(1, 2)), 'gx')  24.8 us
    ppermute x8, starting transfers between devices, with_halo(): lax.ppermute(lax.slice_in_dim(block, block.shape[dim] - width, None, axis...  20.5 us
    ppermute x8, starting transfers between devices, with_halo(): lax.ppermute(lax.slice_in_dim(block, 0, width, axis=dim), axis, backward)  16.8 us
    ppermute x8, waiting for transfers between devices, with_halo(): lax.ppermute(lax.slice_in_dim(block, 0, width, axis=dim), axis, backward)  13.8 us
    ppermute x8, waiting for transfers between devices, with_halo(): lax.ppermute(lax.slice_in_dim(block, block.shape[dim] - width, None, axis...  4.85 us
  transfers between devices with their start and end apart: 16, of which 6 were waited for; matrix products, arithmetic and copies ran while one was open for 4% of the time, Pallas kernels for 0%

commit v1 on v0

v1 whole, which is shorter than its diff:
```python
import functools
import math

import jax
import jax.numpy as jnp
from jax import lax
from jax.experimental import pallas as pl
from jax.experimental.pallas import tpu as pltpu
from jax.sharding import PartitionSpec as P

MESH = pl.DeviceIdType.MESH
STEPS = 2
TURN_RATE = 0.25
ACCEL_MAX = 0.5
SPEED_BASE = 0.5
SPEED_STEP = 0.25
SPEED_MAX = 1.25
WIND_SCALE = 1.0 / 512.0
CFL_NUMBER = 0.8
OBSTACLE_LEVEL = 1.0
F32 = jnp.float32

LEFT, RIGHT, UP, DOWN = 0, 1, 2, 3
CORNERS = ((1, 1), (1, -1), (-1, 1), (-1, -1))


def limiter(before, here):
    return jnp.maximum(jnp.minimum(before, jnp.maximum(here, 0.0)), jnp.minimum(here, 0.0))


def face_parts(values):
    n = values.shape[0] - 4
    diff = values[1:] - values[:-1]
    half = 0.5 * diff
    curve = half[1:] - half[:-1]
    limited = limiter(curve[:-1], curve[1:])
    inner = diff[1 : n + 2]
    return inner[:n] + limited[:n], inner[1:] - limited[1:]


def lane_parts(values):
    lanes = lax.broadcasted_iota(jnp.int32, values.shape, values.ndim - 1)
    axis, extent = values.ndim - 1, values.shape[-1]
    diff = values - pltpu.roll(values, 1, axis)
    after = pltpu.roll(diff, extent - 1, axis)
    diff = jnp.where(lanes == 0, after, diff)
    after = jnp.where(lanes == extent - 1, diff, after)
    curve = 0.5 * (after - diff)
    limited = limiter(pltpu.roll(curve, 1, axis), curve)
    return diff + limited, after - pltpu.roll(limited, extent - 1, axis)


def heading_term(here, other):
    rows = lax.broadcasted_iota(jnp.int32, here.shape, here.ndim - 2)
    axis = here.ndim - 2
    low2 = pltpu.roll(jnp.where(rows >= 6, other, here), 2, axis)
    low1 = pltpu.roll(jnp.where(rows == 7, other, here), 1, axis)
    up1 = pltpu.roll(jnp.where(rows == 0, other, here), 7, axis)
    up2 = pltpu.roll(jnp.where(rows <= 1, other, here), 6, axis)
    diff0, diff1, diff2, diff3 = low1 - low2, here - low1, up1 - here, up2 - up1
    curve0, curve1, curve2 = 0.5 * (diff1 - diff0), 0.5 * (diff2 - diff1), 0.5 * (diff3 - diff2)
    return jnp.maximum(limiter(curve0, curve1) + diff1, limiter(curve1, curve2) - diff2)


def speed_term(s, values):
    if s == 0:
        return jnp.abs(values[1] - values[0])
    if s == 3:
        return jnp.abs(values[3] - values[2])
    diff1, diff2, diff3 = values[1] - values[0], values[2] - values[1], values[3] - values[2]
    limited = limiter(0.5 * (diff2 - diff1), 0.5 * (diff3 - diff2))
    if s == 1:
        return jnp.maximum(diff1, limited - diff2)
    return jnp.maximum(diff2 + limited, -diff3)


def kernel(
    n_gx, n_ha, field_hbm, wind_hbm, obstacle_hbm, out_hbm,
    v_a, w_a, v_b, w_b, sec_t, sec_w, wind_int, wind_f, obst, peaks, trig, out_v,
    send_sem, recv_sem, wind_send, wind_recv, local_sem,
):
    gx, ha = lax.axis_index("gx"), lax.axis_index("ha")
    head_step = 2.0 * math.pi / (8 * n_ha)

    loads = [
        pltpu.make_async_copy(wind_hbm, wind_int.at[:, :, 2:6], local_sem.at[0]),
        pltpu.make_async_copy(field_hbm, v_a.at[:, 4:8], local_sem.at[1]),
        pltpu.make_async_copy(obstacle_hbm, obst, local_sem.at[2]),
    ]
    for copy in loads:
        copy.start()

    def has(dx):
        return (gx + dx >= 0) & (gx + dx < n_gx)

    barrier = pltpu.get_barrier_semaphore()
    for k in range(1, n_gx):
        pl.semaphore_signal(barrier, inc=1, device_id=(lax.rem(gx + k, n_gx), ha), device_id_type=MESH)
    for dh in (1, n_ha - 1):
        pl.semaphore_signal(barrier, inc=1, device_id=(gx, lax.rem(ha + dh, n_ha)), device_id_type=MESH)
    for dx in (1, -1):
        @pl.when(has(dx))
        def _():
            for dh in (1, n_ha - 1):
                pl.semaphore_signal(
                    barrier, inc=1, device_id=(gx + dx, lax.rem(ha + dh, n_ha)), device_id_type=MESH
                )

    loads[0].wait()
    for step in range(STEPS):
        for part in range(2):
            own = jnp.abs(wind_int[step, part, 2:6, :].astype(F32) * WIND_SCALE)
            peaks[n_gx - 1, pl.ds(2 * step + part, 1), :] = jnp.max(own, axis=0, keepdims=True)
    rows = lax.broadcasted_iota(jnp.int32, (8, 128), 0)
    total = 8 * n_ha
    for tile in range(2):
        place = rows if tile == 0 else jnp.where(rows < 4, rows + 8, rows - 8)
        place = lax.rem(ha * 8 + place + total, total)
        angle = place.astype(F32) * head_step
        trig[tile, 0] = jnp.cos(angle)
        trig[tile, 1] = jnp.sin(angle)
    loads[1].wait()

    pl.semaphore_wait(
        barrier, n_gx + 1 + 2 * (has(1).astype(jnp.int32) + has(-1).astype(jnp.int32))
    )

    def remote(src, dst, index, dx, dh):
        return pltpu.make_async_remote_copy(
            src_ref=src, dst_ref=dst, send_sem=send_sem.at[index], recv_sem=recv_sem.at[index],
            device_id=(gx + dx, lax.rem(ha + dh + n_ha, n_ha)), device_id_type=MESH,
        )

    def halo(v, w, base):
        copies = [
            (0, remote(v.at[:, 4:8, 4:8], w.at[:, 2:6, 4:8], base, 0, 1)),
            (0, remote(v.at[:, 4:8, 0:4], w.at[:, 2:6, 0:4], base + 1, 0, -1)),
        ]
        for n, (dx, dh) in enumerate(CORNERS):
            band = slice(6, 8) if dh > 0 else slice(0, 2)
            near, far = (slice(6, 8), slice(0, 2)) if dx > 0 else (slice(4, 6), slice(6, 8))
            copies.append((dx, remote(v.at[:, near, band], w.at[:, far, band], base + 2 + n, dx, dh)))
        copies.append((1, remote(v.at[:, 4:8], v.at[:, 0:4], base + 6, 1, 0)))
        copies.append((-1, remote(v.at[:, 4:8], v.at[:, 8:12], base + 7, -1, 0)))
        return copies

    def at(dx, action):
        if dx == 0:
            action()
        else:
            pl.when(has(dx))(action)

    first = halo(v_a, w_a, 0)
    second = halo(v_b, w_b, 8)
    wind_edges = [
        (1, remote(wind_int.at[:, :, 4:6], wind_int.at[:, :, 0:2], 16, 1, 0)),
        (-1, remote(wind_int.at[:, :, 2:4], wind_int.at[:, :, 6:8], 17, -1, 0)),
    ]
    wind_copies = [
        pltpu.make_async_remote_copy(
            src_ref=peaks.at[n_gx - 1], dst_ref=peaks.at[k - 1],
            send_sem=wind_send.at[k - 1], recv_sem=wind_recv.at[k - 1],
            device_id=(lax.rem(gx + k, n_gx), ha), device_id_type=MESH,
        )
        for k in range(1, n_gx)
    ]
    for dx, copy in first[:2]:
        at(dx, copy.start)
    for copy in wind_copies:
        copy.start()
    for dx, copy in first[2:] + wind_edges:
        at(dx, copy.start)

    for dx, copy in wind_edges:
        at(-dx, copy.wait_recv)
    for step in range(STEPS):
        for part in range(2):
            for plane in range(8):
                row = wind_int[step, part, pl.ds(plane, 1), :].astype(F32) * WIND_SCALE
                wind_f[step, part, plane] = jnp.broadcast_to(row, (8, 128))
    for copy in wind_copies:
        copy.wait_recv()
    highest = jnp.max(peaks[...], axis=0)
    highest = jnp.max(highest, axis=1, keepdims=True)
    alphas, halves = [], []
    for step in range(STEPS):
        pair = [
            jnp.broadcast_to(SPEED_MAX + highest[2 * step + part : 2 * step + part + 1], (8, 128))
            for part in range(2)
        ]
        alphas.append(pair)
        halves.append(
            (0.5 * CFL_NUMBER)
            / (pair[0] + pair[1] + (TURN_RATE / head_step + ACCEL_MAX / SPEED_STEP))
        )

    def gain(step, s, tile, first_plane, around_x, here, other, speeds_here):
        speed = SPEED_BASE + SPEED_STEP * s
        alpha_x, alpha_y = alphas[step]
        back, fore = face_parts(around_x)
        velocity = speed * trig[tile, 0] + wind_f[step, 0, first_plane : first_plane + 4]
        result = (back + fore) * velocity + alpha_x * (fore - back)
        back, fore = lane_parts(here)
        velocity = speed * trig[tile, 1] + wind_f[step, 1, first_plane : first_plane + 4]
        result = result + (back + fore) * velocity + alpha_y * (fore - back)
        result = result - (2.0 * TURN_RATE / head_step) * heading_term(here, other)
        return result - (2.0 * ACCEL_MAX / SPEED_STEP) * speed_term(s, speeds_here)

    def advance(step, v, w, finish):
        half = halves[step]

        def ends(ref, low, count):
            @pl.when(gx == 0)
            def _():
                a, b = ref[:, low], ref[:, low + 1]
                ref[:, low - 1] = 2.0 * a - b
                ref[:, low - 2] = 3.0 * a - 2.0 * b

            @pl.when(gx == n_gx - 1)
            def _():
                a, b = ref[:, low + count - 1], ref[:, low + count - 2]
                ref[:, low + count] = 2.0 * a - b
                ref[:, low + count + 1] = 3.0 * a - 2.0 * b

        ends(v, 4, 4)
        ends(w, 2, 4)
        for s in range(4):
            for block in (0, 4):
                here = v[s, block + 2 : block + 6]
                speeds = [v[i, block + 2 : block + 6] for i in range(4)]
                sec_t[s, block : block + 4] = here + half * gain(
                    step, s, 0, block, v[s, block : block + 8], here, w[s, block : block + 4], speeds
                )
            here = w[s, 2:6]
            speeds = [w[i, 2:6] for i in range(4)]
            sec_w[s] = here + half * gain(step, s, 1, 2, w[s], here, v[s, 4:8], speeds)
        ends(sec_t, 2, 4)
        for s in range(4):
            here = sec_t[s, 2:6]
            speeds = [sec_t[i, 2:6] for i in range(4)]
            change = half * gain(step, s, 0, 2, sec_t[s], here, sec_w[s], speeds)
            finish(s, 0.5 * (v[s, 4:8] + (here + change)))

    def limit(s, candidate, plane):
        blocked = jnp.broadcast_to(obst[pl.ds(plane, 1), :], (8, 128)) == 1
        value = candidate[plane]
        return jnp.where(blocked, jnp.maximum(value, OBSTACLE_LEVEL), value)

    def keep(s, candidate):
        for plane in range(4):
            v_b[s, 4 + plane] = limit(s, candidate, plane)

    def give(s, candidate):
        for plane in range(4):
            out_v[s, plane] = limit(s, candidate, plane)

    for dx, copy in first:
        at(-dx, copy.wait_recv)
    loads[2].wait()
    advance(0, v_a, w_a, keep)
    for dx, copy in second:
        at(dx, copy.start)
    for dx, copy in first + wind_edges:
        at(dx, copy.wait_send)
    for copy in wind_copies:
        copy.wait_send()
    for dx, copy in second:
        at(-dx, copy.wait_recv)
    advance(1, v_b, w_b, give)
    result = pltpu.make_async_copy(out_v, out_hbm, local_sem.at[3])
    result.start()
    for dx, copy in second:
        at(dx, copy.wait_send)
    result.wait()


def solution(mesh):
    n_gx, n_ha = mesh.shape["gx"], mesh.shape["ha"]

    def local(value_field, wind_grid, obstacle):
        return pl.pallas_call(
            functools.partial(kernel, n_gx, n_ha),
            out_shape=jax.ShapeDtypeStruct(value_field.shape, F32),
            in_specs=[pl.BlockSpec(memory_space=pl.ANY)] * 3,
            out_specs=pl.BlockSpec(memory_space=pl.ANY),
            scratch_shapes=[
                pltpu.VMEM((4, 12, 8, 128), F32),
                pltpu.VMEM((4, 8, 8, 128), F32),
                pltpu.VMEM((4, 12, 8, 128), F32),
                pltpu.VMEM((4, 8, 8, 128), F32),
                pltpu.VMEM((4, 8, 8, 128), F32),
                pltpu.VMEM((4, 4, 8, 128), F32),
                pltpu.VMEM((2, 2, 8, 128), jnp.int32),
                pltpu.VMEM((2, 2, 8, 8, 128), F32),
                pltpu.VMEM((4, 128), jnp.int32),
                pltpu.VMEM((n_gx, 4, 128), F32),
                pltpu.VMEM((2, 2, 8, 128), F32),
                pltpu.VMEM((4, 4, 8, 128), F32),
                pltpu.SemaphoreType.DMA((18,)),
                pltpu.SemaphoreType.DMA((18,)),
                pltpu.SemaphoreType.DMA((n_gx - 1,)),
                pltpu.SemaphoreType.DMA((n_gx - 1,)),
                pltpu.SemaphoreType.DMA((4,)),
            ],
            compiler_params=pltpu.CompilerParams(collective_id=0, has_side_effects=True),
            name="reach",
        )(value_field, wind_grid, obstacle)

    placed = (P(None, "gx", "ha", None), P(None, None, "gx", None), P("gx", None))
    return jax.shard_map(
        local, mesh=mesh, in_specs=placed, out_specs=P(None, "gx", "ha", None), check_vma=False
    )
```

time: 92.5 us -> 25.4 us (0.27)
  the two profiles are of different devices: /device:TPU:88 before, /device:TPU:1 now
where the time goes in v1:
time: 25.4 us; the launch traced here: 25.3 us
  Pallas kernels  23.8 us (94%)
  local copies, waits for them, and re-layouts  1.47 us (6%)
    pallas_call x1, Pallas kernels, local(): pl.pallas_call(functools.partial(kernel, n_gx, n_ha), out_shape=jax.Shape...  23.8 us
    unnamed x1, local copies, waits for them, and re-layouts  1.47 us

profile of v1, /device:TPU:1, one launch (start us, length us, event | category | flops | bytes accessed | tf_op | source)
XLA Modules:
  0.0 25.3 jit_solution(7209868824817924341)
XLA Ops:
  0.0 23.8 %reach.1 = f32[4,4,8,128]{3,2,1,0:T(8,128)} custom-call(f32[4,4,8,128]{3,2,1,0:T(8,128)} %field_hbm.1, s32[2,2,4,128]{3,2,1,0:T(4,128)} %wind_hbm.1, s32[4,128]{1,0:T(4,128)} %obstacle_hbm.1), custom_call_target="tpu_custom_call" | custom-call | tf_op jit(solution)/shard_map/reach/pallas_call | solution.py:281
  23.8 1.5 %copy.5 = f32[4,4,8,128]{3,2,1,0:T(8,128)} copy(f32[4,4,8,128]{3,2,1,0:T(8,128)} %reach.1) | data formatting | bytes 131072

commit v2 on v1

v2 whole, which is shorter than its diff:
```python
import functools
import math

import jax
import jax.numpy as jnp
from jax import lax
from jax.experimental import pallas as pl
from jax.experimental.pallas import tpu as pltpu
from jax.sharding import PartitionSpec as P

MESH = pl.DeviceIdType.MESH
STEPS = 2
TURN_RATE = 0.25
ACCEL_MAX = 0.5
SPEED_BASE = 0.5
SPEED_STEP = 0.25
SPEED_MAX = 1.25
WIND_SCALE = 1.0 / 512.0
CFL_NUMBER = 0.8
OBSTACLE_LEVEL = 1.0
F32 = jnp.float32

CORNERS = ((1, 1), (1, -1), (-1, 1), (-1, -1))


def limiter(before, here):
    return jnp.maximum(jnp.minimum(before, jnp.maximum(here, 0.0)), jnp.minimum(here, 0.0))


def parts(diff0, diff1, diff2, diff3):
    curve = diff2 - diff1
    backward = diff1 + 0.5 * limiter(diff1 - diff0, curve)
    forward = diff2 - 0.5 * limiter(curve, diff3 - diff2)
    return backward, forward


def plane_parts(values):
    n = values.shape[1] - 4
    diff = values[:, 1:] - values[:, :-1]
    curve = diff[:, 1:] - diff[:, :-1]
    limited = 0.5 * limiter(curve[:, :-1], curve[:, 1:])
    inner = diff[:, 1 : n + 2]
    return inner[:, :n] + limited[:, :n], inner[:, 1:] - limited[:, 1:]


def lane_parts(here):
    axis, extent = here.ndim - 1, here.shape[-1]
    lanes = lax.broadcasted_iota(jnp.int32, here.shape, axis)
    low1, low2 = pltpu.roll(here, 1, axis), pltpu.roll(here, 2, axis)
    up1, up2 = pltpu.roll(here, extent - 1, axis), pltpu.roll(here, extent - 2, axis)
    below, above = here - low1, up1 - here
    diff1 = jnp.where(lanes == 0, above, below)
    diff2 = jnp.where(lanes == extent - 1, below, above)
    diff0 = jnp.where(lanes <= 1, diff1, low1 - low2)
    diff3 = jnp.where(lanes >= extent - 2, diff2, up2 - up1)
    return parts(diff0, diff1, diff2, diff3)


def heading_term(here, other):
    axis = here.ndim - 2
    rows = lax.broadcasted_iota(jnp.int32, here.shape, axis)
    low2 = pltpu.roll(jnp.where(rows >= 6, other, here), 2, axis)
    low1 = pltpu.roll(jnp.where(rows == 7, other, here), 1, axis)
    up1 = pltpu.roll(jnp.where(rows == 0, other, here), 7, axis)
    up2 = pltpu.roll(jnp.where(rows <= 1, other, here), 6, axis)
    backward, forward = parts(low1 - low2, here - low1, up1 - here, up2 - up1)
    return jnp.maximum(backward, -forward)


def speed_terms(values):
    diff = [values[i + 1] - values[i] for i in range(3)]
    limited = 0.5 * limiter(diff[1] - diff[0], diff[2] - diff[1])
    return jnp.stack([
        jnp.abs(diff[0]),
        jnp.maximum(diff[0], limited - diff[1]),
        jnp.maximum(diff[1] + limited, -diff[2]),
        jnp.abs(diff[2]),
    ])


def kernel(
    n_gx, n_ha, field_hbm, wind_hbm, obstacle_hbm, out_v,
    v_a, w_a, v_b, w_b, sec_t, sec_w, known, jump_x, jump_y, wind_int, wind_f, obst, peaks, drift,
    send_sem, recv_sem, wind_send, wind_recv, local_sem,
):
    gx, ha = lax.axis_index("gx"), lax.axis_index("ha")
    head_step = 2.0 * math.pi / (8 * n_ha)

    loads = [
        pltpu.make_async_copy(wind_hbm, wind_int.at[:, :, 2:6], local_sem.at[0]),
        pltpu.make_async_copy(field_hbm, v_a.at[:, 4:8], local_sem.at[1]),
        pltpu.make_async_copy(obstacle_hbm, obst, local_sem.at[2]),
    ]
    for copy in loads:
        copy.start()

    def has(dx):
        return (gx + dx >= 0) & (gx + dx < n_gx)

    barrier = pltpu.get_barrier_semaphore()
    for k in range(1, n_gx):
        pl.semaphore_signal(barrier, inc=1, device_id=(lax.rem(gx + k, n_gx), ha), device_id_type=MESH)
    for dh in (1, n_ha - 1):
        pl.semaphore_signal(barrier, inc=1, device_id=(gx, lax.rem(ha + dh, n_ha)), device_id_type=MESH)
    for dx in (1, -1):
        @pl.when(has(dx))
        def _():
            for dh in (1, n_ha - 1):
                pl.semaphore_signal(
                    barrier, inc=1, device_id=(gx + dx, lax.rem(ha + dh, n_ha)), device_id_type=MESH
                )

    loads[0].wait()
    for step in range(STEPS):
        for part in range(2):
            own = jnp.abs(wind_int[step, part, 2:6, :].astype(F32) * WIND_SCALE)
            peaks[n_gx - 1, pl.ds(2 * step + part, 1), :] = jnp.max(own, axis=0, keepdims=True)
    rows = lax.broadcasted_iota(jnp.int32, (8, 128), 0)
    total = 8 * n_ha
    for tile in range(2):
        place = rows if tile == 0 else jnp.where(rows < 4, rows + 8, rows - 8)
        place = lax.rem(ha * 8 + place + total, total)
        angle = place.astype(F32) * head_step
        for part, value in enumerate((jnp.cos(angle), jnp.sin(angle))):
            for s in range(4):
                drift[tile, part, s] = (SPEED_BASE + SPEED_STEP * s) * value
    loads[1].wait()

    pl.semaphore_wait(
        barrier, n_gx + 1 + 2 * (has(1).astype(jnp.int32) + has(-1).astype(jnp.int32))
    )

    def remote(src, dst, index, dx, dh):
        return pltpu.make_async_remote_copy(
            src_ref=src, dst_ref=dst, send_sem=send_sem.at[index], recv_sem=recv_sem.at[index],
            device_id=(gx + dx, lax.rem(ha + dh + n_ha, n_ha)), device_id_type=MESH,
        )

    def halo(v, w, base, part):
        copies = [
            (0, remote(v.at[part, 4:8, 4:8], w.at[part, 2:6, 4:8], base, 0, 1)),
            (0, remote(v.at[part, 4:8, 0:4], w.at[part, 2:6, 0:4], base + 1, 0, -1)),
        ]
        for n, (dx, dh) in enumerate(CORNERS):
            band = slice(6, 8) if dh > 0 else slice(0, 2)
            near, far = (slice(6, 8), slice(0, 2)) if dx > 0 else (slice(4, 6), slice(6, 8))
            copies.append((dx, remote(v.at[part, near, band], w.at[part, far, band], base + 2 + n, dx, dh)))
        copies.append((1, remote(v.at[part, 4:8], v.at[part, 0:4], base + 6, 1, 0)))
        copies.append((-1, remote(v.at[part, 4:8], v.at[part, 8:12], base + 7, -1, 0)))
        return copies

    def start(copies):
        for dx in (0, 1, -1):
            mine = [copy for d, copy in copies if d == dx]

            def run(mine=mine):
                for copy in mine:
                    copy.start()

            guarded(dx, mine, run)

    def receive(copies):
        for dx in (0, 1, -1):
            mine = [copy for d, copy in copies if d == dx]

            def run(mine=mine):
                for copy in mine:
                    copy.wait_recv()

            guarded(-dx, mine, run)

    def finish_sends(copies):
        for dx in (0, 1, -1):
            mine = [copy for d, copy in copies if d == dx]

            def run(mine=mine):
                for copy in mine:
                    copy.wait_send()

            guarded(dx, mine, run)

    def guarded(dx, mine, run):
        if not mine:
            return
        if dx == 0:
            run()
        else:
            pl.when(has(dx))(run)

    first = halo(v_a, w_a, 0, slice(0, 4))
    second = halo(v_b, w_b, 10, slice(0, 4))
    wind_edges = [
        (1, remote(wind_int.at[:, :, 4:6], wind_int.at[:, :, 0:2], 8, 1, 0)),
        (-1, remote(wind_int.at[:, :, 2:4], wind_int.at[:, :, 6:8], 9, -1, 0)),
    ]
    wind_copies = [
        pltpu.make_async_remote_copy(
            src_ref=peaks.at[n_gx - 1], dst_ref=peaks.at[k - 1],
            send_sem=wind_send.at[k - 1], recv_sem=wind_recv.at[k - 1],
            device_id=(lax.rem(gx + k, n_gx), ha), device_id_type=MESH,
        )
        for k in range(1, n_gx)
    ]
    start(first[:2])
    for copy in wind_copies:
        copy.start()
    start(first[2:] + wind_edges)

    half_scale = ACCEL_MAX / SPEED_STEP * 2.0
    head_scale = 2.0 * TURN_RATE / head_step
    own, left, right = slice(4, 8), slice(2, 4), slice(8, 10)

    def ends(ref, low, count):
        for at_end, edge, next_one, near, far in (
            (gx == 0, low, low + 1, low - 1, low - 2),
            (gx == n_gx - 1, low + count - 1, low + count - 2, low + count, low + count + 1),
        ):
            a, b = ref[:, edge], ref[:, next_one]
            ref[:, near] = jnp.where(at_end, 2.0 * a - b, ref[:, near])
            ref[:, far] = jnp.where(at_end, 3.0 * a - 2.0 * b, ref[:, far])

    def across(step, tile, planes, here):
        back, fore = lane_parts(here)
        velocity = drift[tile, 1][:, None] + wind_f[step, 1, planes][None]
        return (back + fore) * velocity, fore - back

    def along(step, tile, planes, around):
        back, fore = plane_parts(around)
        velocity = drift[tile, 0][:, None] + wind_f[step, 0, planes][None]
        return (back + fore) * velocity, fore - back

    def begin(step, v, planes):
        place = slice(planes.start - 2, planes.stop - 2)
        values = v[:, planes]
        mean, jump = across(step, 0, place, values)
        known[:, place] = mean - half_scale * speed_terms(values)
        jump_y[:, place] = jump

    def extend_x(step, v):
        for block in (0, 4):
            place = slice(block, block + 4)
            mean, jump = along(step, 0, place, v[:, block : block + 8])
            known[:, place] = known[:, place] + mean
            jump_x[:, place] = jump

    def whole(step, tile, planes, around, here, other):
        alpha_x, alpha_y = alphas[step]
        mean_x, jump_at_x = along(step, tile, planes, around)
        mean_y, jump_at_y = across(step, tile, planes, here)
        result = mean_x + mean_y + alpha_x * jump_at_x + alpha_y * jump_at_y
        return halves[step] * (
            result - head_scale * heading_term(here, other) - half_scale * speed_terms(here)
        )

    def first_stage(step, v, w):
        alpha_x, alpha_y = alphas[step]
        for block in (0, 4):
            place = slice(block, block + 4)
            here, other = v[:, block + 2 : block + 6], w[:, place]
            rest = known[:, place] + alpha_x * jump_x[:, place] + alpha_y * jump_y[:, place]
            sec_t[:, place] = here + halves[step] * (rest - head_scale * heading_term(here, other))
        here = w[:, 2:6]
        sec_w[...] = here + whole(step, 1, slice(2, 6), w[...], here, v[:, own])

    def second_stage(step, v, finish):
        ends(sec_t, 2, 4)
        here = sec_t[:, 2:6]
        change = whole(step, 0, slice(2, 6), sec_t[...], here, sec_w[...])
        finish(0.5 * (v[:, own] + (here + change)))

    def limit(candidate, plane):
        blocked = jnp.broadcast_to(obst[pl.ds(plane, 1), :], (8, 128)) == 1
        value = candidate[:, plane]
        return jnp.where(blocked[None], jnp.maximum(value, OBSTACLE_LEVEL), value)

    def keep(candidate):
        for plane in range(4):
            v_b[:, 4 + plane] = limit(candidate, plane)
        start(second)

    def give(candidate):
        for plane in range(4):
            out_v[:, plane] = limit(candidate, plane)

    def spread(planes):
        for step in range(STEPS):
            for part in range(2):
                for plane in planes:
                    row = wind_int[step, part, pl.ds(plane, 1), :].astype(F32) * WIND_SCALE
                    wind_f[step, part, plane] = jnp.broadcast_to(row, (8, 128))

    spread(range(2, 6))
    begin(0, v_a, own)
    receive(wind_edges + first[6:])
    spread((0, 1, 6, 7))
    ends(v_a, 4, 4)
    begin(0, v_a, left)
    begin(0, v_a, right)
    extend_x(0, v_a)

    for copy in wind_copies:
        copy.wait_recv()
    highest = jnp.max(peaks[...], axis=0)
    highest = jnp.max(highest, axis=1, keepdims=True)
    alphas, halves = [], []
    for step in range(STEPS):
        pair = [
            jnp.broadcast_to(SPEED_MAX + highest[2 * step + part : 2 * step + part + 1], (8, 128))
            for part in range(2)
        ]
        alphas.append(pair)
        halves.append(
            (0.5 * CFL_NUMBER)
            / (pair[0] + pair[1] + (TURN_RATE / head_step + ACCEL_MAX / SPEED_STEP))
        )

    receive(first[:6])
    loads[2].wait()
    ends(w_a, 2, 4)
    first_stage(0, v_a, w_a)
    second_stage(0, v_a, keep)

    begin(1, v_b, own)
    receive(second[6:])
    ends(v_b, 4, 4)
    begin(1, v_b, left)
    begin(1, v_b, right)
    extend_x(1, v_b)
    receive(second[:6])
    ends(w_b, 2, 4)
    first_stage(1, v_b, w_b)
    second_stage(1, v_b, give)
    finish_sends(first + wind_edges + second)
    for copy in wind_copies:
        copy.wait_send()


def solution(mesh):
    n_gx, n_ha = mesh.shape["gx"], mesh.shape["ha"]

    def local(value_field, wind_grid, obstacle):
        return pl.pallas_call(
            functools.partial(kernel, n_gx, n_ha),
            out_shape=jax.ShapeDtypeStruct(value_field.shape, F32),
            in_specs=[pl.BlockSpec(memory_space=pltpu.HBM)] * 3,
            out_specs=pl.BlockSpec(memory_space=pltpu.VMEM),
            scratch_shapes=[
                pltpu.VMEM((4, 12, 8, 128), F32),
                pltpu.VMEM((4, 8, 8, 128), F32),
                pltpu.VMEM((4, 12, 8, 128), F32),
                pltpu.VMEM((4, 8, 8, 128), F32),
                pltpu.VMEM((4, 8, 8, 128), F32),
                pltpu.VMEM((4, 4, 8, 128), F32),
                pltpu.VMEM((4, 8, 8, 128), F32),
                pltpu.VMEM((4, 8, 8, 128), F32),
                pltpu.VMEM((4, 8, 8, 128), F32),
                pltpu.VMEM((2, 2, 8, 128), jnp.int32),
                pltpu.VMEM((2, 2, 8, 8, 128), F32),
                pltpu.VMEM((4, 128), jnp.int32),
                pltpu.VMEM((n_gx, 4, 128), F32),
                pltpu.VMEM((2, 2, 4, 8, 128), F32),
                pltpu.SemaphoreType.DMA((18,)),
                pltpu.SemaphoreType.DMA((18,)),
                pltpu.SemaphoreType.DMA((n_gx - 1,)),
                pltpu.SemaphoreType.DMA((n_gx - 1,)),
                pltpu.SemaphoreType.DMA((4,)),
            ],
            compiler_params=pltpu.CompilerParams(collective_id=0, has_side_effects=True, vmem_limit_bytes=8 * 1024 * 1024),
            name="reach",
        )(*[pltpu.with_memory_space_constraint(x, pltpu.HBM) for x in (value_field, wind_grid, obstacle)])

    placed = (P(None, "gx", "ha", None), P(None, None, "gx", None), P("gx", None))
    return jax.shard_map(
        local, mesh=mesh, in_specs=placed, out_specs=P(None, "gx", "ha", None), check_vma=False
    )
```

time: 25.4 us -> 23.3 us (0.917)
  Pallas kernels: 23.8 us -> 22.5 us
  local copies, waits for them, and re-layouts: 1.47 us -> 0.63 us
    pallas_call x1, Pallas kernels: 23.8 us -> 22.5 us  [local(): pl.pallas_call(functools.partial(kernel, n_gx, n_ha), out_shape=jax.Shape...]
    unnamed x1, local copies, waits for them, and re-layouts: 1.47 us -> 0.63 us
where the time goes in v2:
time: 23.3 us; the launch traced here: 23.2 us
  Pallas kernels  22.5 us (97%)
  local copies, waits for them, and re-layouts  0.63 us (3%)
    pallas_call x1, Pallas kernels, local(): pl.pallas_call(functools.partial(kernel, n_gx, n_ha), out_shape=jax.Shape...  22.5 us
    unnamed x1, local copies, waits for them, and re-layouts  0.63 us

profile of v2, /device:TPU:1, one launch (start us, length us, event | category | flops | bytes accessed | tf_op | source)
XLA Modules:
  0.0 23.2 jit_solution(2331272284354162249)
XLA Ops:
  0.0 22.5 %reach.1 = f32[4,4,8,128]{3,2,1,0:T(8,128)S(1)} custom-call(f32[4,4,8,128]{3,2,1,0:T(8,128)} %field_hbm.1, s32[2,2,4,128]{3,2,1,0:T(4,128)} %wind_hbm.1, s32[4,128]{1,0:T(4,128)} %obstacle_hbm.1), custom_call_target="tpu_custom_call" | custom-call | tf_op jit(solution)/shard_map/reach/pallas_call | solution.py:342
  22.5 0.6 %copy.5 = f32[4,4,8,128]{3,2,1,0:T(8,128)} copy(f32[4,4,8,128]{3,2,1,0:T(8,128)S(1)} %reach.1) | data formatting | bytes 131072

commit v3 on v2

--- a/solution.py
+++ b/solution.py
@@ -20,8 +20,6 @@
 OBSTACLE_LEVEL = 1.0
 F32 = jnp.float32
 
-CORNERS = ((1, 1), (1, -1), (-1, 1), (-1, -1))
-
 
 def limiter(before, here):
     return jnp.maximum(jnp.minimum(before, jnp.maximum(here, 0.0)), jnp.minimum(here, 0.0))
@@ -81,15 +79,16 @@
 def kernel(
     n_gx, n_ha, field_hbm, wind_hbm, obstacle_hbm, out_v,
     v_a, w_a, v_b, w_b, sec_t, sec_w, known, jump_x, jump_y, wind_int, wind_f, obst, peaks, drift,
-    send_sem, recv_sem, wind_send, wind_recv, local_sem,
+    send_sem, recv_sem, wind_send, wind_recv, ready, local_sem,
 ):
     gx, ha = lax.axis_index("gx"), lax.axis_index("ha")
     head_step = 2.0 * math.pi / (8 * n_ha)
 
     loads = [
         pltpu.make_async_copy(wind_hbm, wind_int.at[:, :, 2:6], local_sem.at[0]),
-        pltpu.make_async_copy(field_hbm, v_a.at[:, 4:8], local_sem.at[1]),
-        pltpu.make_async_copy(obstacle_hbm, obst, local_sem.at[2]),
+        pltpu.make_async_copy(field_hbm.at[:, :, 0:4], v_a.at[:, 4:8, 4:8], local_sem.at[1]),
+        pltpu.make_async_copy(field_hbm.at[:, :, 4:8], w_a.at[:, 2:6, 0:4], local_sem.at[2]),
+        pltpu.make_async_copy(obstacle_hbm, obst, local_sem.at[3]),
     ]
     for copy in loads:
         copy.start()
@@ -97,37 +96,39 @@
     def has(dx):
         return (gx + dx >= 0) & (gx + dx < n_gx)
 
+    below, above = lax.rem(ha + n_ha - 1, n_ha), lax.rem(ha + 1, n_ha)
     barrier = pltpu.get_barrier_semaphore()
-    for k in range(1, n_gx):
-        pl.semaphore_signal(barrier, inc=1, device_id=(lax.rem(gx + k, n_gx), ha), device_id_type=MESH)
-    for dh in (1, n_ha - 1):
-        pl.semaphore_signal(barrier, inc=1, device_id=(gx, lax.rem(ha + dh, n_ha)), device_id_type=MESH)
+
+    def signal(semaphore, x, h):
+        pl.semaphore_signal(semaphore, inc=1, device_id=(x, h), device_id_type=MESH)
+
+    signal(barrier, gx, below)
     for dx in (1, -1):
-        @pl.when(has(dx))
-        def _():
-            for dh in (1, n_ha - 1):
-                pl.semaphore_signal(
-                    barrier, inc=1, device_id=(gx + dx, lax.rem(ha + dh, n_ha)), device_id_type=MESH
-                )
+        pl.when(has(dx))(functools.partial(signal, barrier, gx + dx, below))
+
+    @pl.loop(gx + 1, n_gx)
+    def _(k):
+        signal(barrier, k, ha)
 
     loads[0].wait()
     for step in range(STEPS):
         for part in range(2):
             own = jnp.abs(wind_int[step, part, 2:6, :].astype(F32) * WIND_SCALE)
-            peaks[n_gx - 1, pl.ds(2 * step + part, 1), :] = jnp.max(own, axis=0, keepdims=True)
+            peaks[gx, pl.ds(2 * step + part, 1), :] = jnp.max(own, axis=0, keepdims=True)
     rows = lax.broadcasted_iota(jnp.int32, (8, 128), 0)
     total = 8 * n_ha
     for tile in range(2):
         place = rows if tile == 0 else jnp.where(rows < 4, rows + 8, rows - 8)
-        place = lax.rem(ha * 8 + place + total, total)
-        angle = place.astype(F32) * head_step
-        for part, value in enumerate((jnp.cos(angle), jnp.sin(angle))):
-            for s in range(4):
-                drift[tile, part, s] = (SPEED_BASE + SPEED_STEP * s) * value
+        for step in range(STEPS):
+            angle = lax.rem(ha * 8 + place + (total - 4 + 4 * step), total).astype(F32) * head_step
+            for part, value in enumerate((jnp.cos(angle), jnp.sin(angle))):
+                for s in range(4):
+                    drift[step, tile, part, s] = (SPEED_BASE + SPEED_STEP * s) * value
     loads[1].wait()
+    loads[2].wait()
 
     pl.semaphore_wait(
-        barrier, n_gx + 1 + 2 * (has(1).astype(jnp.int32) + has(-1).astype(jnp.int32))
+        barrier, 1 + gx + has(1).astype(jnp.int32) + has(-1).astype(jnp.int32)
     )
 
     def remote(src, dst, index, dx, dh):
@@ -136,18 +137,26 @@
             device_id=(gx + dx, lax.rem(ha + dh + n_ha, n_ha)), device_id_type=MESH,
         )
 
-    def halo(v, w, base, part):
-        copies = [
-            (0, remote(v.at[part, 4:8, 4:8], w.at[part, 2:6, 4:8], base, 0, 1)),
-            (0, remote(v.at[part, 4:8, 0:4], w.at[part, 2:6, 0:4], base + 1, 0, -1)),
+    def halo(v, w, base, way):
+        low, high = slice(0, 4), slice(4, 8)
+        mine, theirs = (high, low) if way > 0 else (low, high)
+        inner, outer = (slice(0, 2), slice(6, 8)) if way > 0 else (slice(6, 8), slice(0, 2))
+        copies, sides = [], ((1, slice(0, 4), slice(6, 8), slice(0, 2)), (-1, slice(8, 12), slice(4, 6), slice(6, 8)))
+        for dx, to, near, far in sides:
+            near_w = slice(near.start - 2, near.stop - 2)
+            copies += [
+                (dx, v.at[:, near, outer], w.at[:, far, outer], way),
+                (dx, w.at[:, 2:6, theirs], v.at[:, to, theirs], way),
+                (dx, w.at[:, near_w, inner], w.at[:, far, inner], 0),
+                (dx, v.at[:, 4:8, mine], v.at[:, to, mine], 0),
+            ]
+        copies = [copies[n] for n in (0, 4, 1, 5)] + [
+            (0, w.at[:, 2:6, theirs], v.at[:, 4:8, theirs], way),
+            (0, v.at[:, 4:8, mine], w.at[:, 2:6, mine], way),
+        ] + [copies[n] for n in (2, 6, 3, 7)]
+        return [
+            (dx, remote(src, dst, base + n, dx, dh)) for n, (dx, src, dst, dh) in enumerate(copies)
         ]
-        for n, (dx, dh) in enumerate(CORNERS):
-            band = slice(6, 8) if dh > 0 else slice(0, 2)
-            near, far = (slice(6, 8), slice(0, 2)) if dx > 0 else (slice(4, 6), slice(6, 8))
-            copies.append((dx, remote(v.at[part, near, band], w.at[part, far, band], base + 2 + n, dx, dh)))
-        copies.append((1, remote(v.at[part, 4:8], v.at[part, 0:4], base + 6, 1, 0)))
-        copies.append((-1, remote(v.at[part, 4:8], v.at[part, 8:12], base + 7, -1, 0)))
-        return copies
 
     def start(copies):
         for dx in (0, 1, -1):
@@ -187,24 +196,37 @@
         else:
             pl.when(has(dx))(run)
 
-    first = halo(v_a, w_a, 0, slice(0, 4))
-    second = halo(v_b, w_b, 10, slice(0, 4))
+    first = halo(v_a, w_a, 0, 1)
+    second = halo(v_b, w_b, 10, -1)
     wind_edges = [
-        (1, remote(wind_int.at[:, :, 4:6], wind_int.at[:, :, 0:2], 8, 1, 0)),
-        (-1, remote(wind_int.at[:, :, 2:4], wind_int.at[:, :, 6:8], 9, -1, 0)),
+        (1, remote(wind_int.at[:, :, 4:6], wind_int.at[:, :, 0:2], 20, 1, 0)),
+        (-1, remote(wind_int.at[:, :, 2:4], wind_int.at[:, :, 6:8], 21, -1, 0)),
     ]
-    wind_copies = [
-        pltpu.make_async_remote_copy(
-            src_ref=peaks.at[n_gx - 1], dst_ref=peaks.at[k - 1],
-            send_sem=wind_send.at[k - 1], recv_sem=wind_recv.at[k - 1],
-            device_id=(lax.rem(gx + k, n_gx), ha), device_id_type=MESH,
+    def wind_copy(k):
+        return pltpu.make_async_remote_copy(
+            src_ref=peaks.at[gx], dst_ref=peaks.at[gx], send_sem=wind_send.at[k], recv_sem=wind_recv.at[gx],
+            device_id=(k, ha), device_id_type=MESH,
         )
-        for k in range(1, n_gx)
-    ]
-    start(first[:2])
-    for copy in wind_copies:
-        copy.start()
-    start(first[2:] + wind_edges)
+
+    def wind_arrival(k):
+        return pltpu.make_async_remote_copy(
+            src_ref=peaks.at[k], dst_ref=peaks.at[k], send_sem=wind_send.at[k], recv_sem=wind_recv.at[k],
+            device_id=(k, ha), device_id_type=MESH,
+        )
+
+    pl.when(has(-1))(lambda: signal(ready.at[0], gx - 1, ha))
+
+    @pl.loop(0, gx)
+    def _(k):
+        signal(ready.at[1], k, ha)
+
+    upward = [copy for n, copy in enumerate(first) if n in (6, 8)] + wind_edges[:1]
+    start(first[:6])
+    start([copy for n, copy in enumerate(first) if n in (7, 9)] + wind_edges[1:])
+
+    @pl.loop(0, gx)
+    def _(k):
+        wind_copy(k).start()
 
     half_scale = ACCEL_MAX / SPEED_STEP * 2.0
     head_scale = 2.0 * TURN_RATE / head_step
@@ -221,12 +243,12 @@
 
     def across(step, tile, planes, here):
         back, fore = lane_parts(here)
-        velocity = drift[tile, 1][:, None] + wind_f[step, 1, planes][None]
+        velocity = drift[step, tile, 1][:, None] + wind_f[step, 1, planes][None]
         return (back + fore) * velocity, fore - back
 
     def along(step, tile, planes, around):
         back, fore = plane_parts(around)
-        velocity = drift[tile, 0][:, None] + wind_f[step, 0, planes][None]
+        velocity = drift[step, tile, 0][:, None] + wind_f[step, 0, planes][None]
         return (back + fore) * velocity, fore - back
 
     def begin(step, v, planes):
@@ -275,7 +297,9 @@
 
     def keep(candidate):
         for plane in range(4):
-            v_b[:, 4 + plane] = limit(candidate, plane)
+            swapped = pltpu.roll(limit(candidate, plane), 4, 1)
+            v_b[:, 4 + plane, 0:4] = swapped[:, 0:4]
+            w_b[:, 2 + plane, 4:8] = swapped[:, 4:8]
         start(second)
 
     def give(candidate):
@@ -290,16 +314,38 @@
                     wind_f[step, part, plane] = jnp.broadcast_to(row, (8, 128))
 
     spread(range(2, 6))
+
+    @pl.when(has(1))
+    def _():
+        pl.semaphore_wait(ready.at[0], 1)
+
+    start(upward)
+
+    @pl.when(gx < n_gx - 1)
+    def _():
+        pl.semaphore_wait(ready.at[1], n_gx - 1 - gx)
+
+    @pl.loop(gx + 1, n_gx)
+    def _(k):
+        wind_copy(k).start()
+
+    receive(wind_edges)
+    spread((0, 1, 6, 7))
+
+    loads[3].wait()
+    receive(first[4:6])
     begin(0, v_a, own)
-    receive(wind_edges + first[6:])
-    spread((0, 1, 6, 7))
+    receive(first[:4] + first[6:])
     ends(v_a, 4, 4)
+    ends(w_a, 2, 4)
     begin(0, v_a, left)
     begin(0, v_a, right)
     extend_x(0, v_a)
 
-    for copy in wind_copies:
-        copy.wait_recv()
+    @pl.loop(0, n_gx - 1)
+    def _(n):
+        wind_arrival(n + (n >= gx).astype(jnp.int32)).wait_recv()
+
     highest = jnp.max(peaks[...], axis=0)
     highest = jnp.max(highest, axis=1, keepdims=True)
     alphas, halves = [], []
@@ -314,25 +360,24 @@
             / (pair[0] + pair[1] + (TURN_RATE / head_step + ACCEL_MAX / SPEED_STEP))
         )
 
-    receive(first[:6])
-    loads[2].wait()
-    ends(w_a, 2, 4)
     first_stage(0, v_a, w_a)
     second_stage(0, v_a, keep)
 
+    receive(second[4:6])
     begin(1, v_b, own)
-    receive(second[6:])
+    receive(second[:4] + second[6:])
     ends(v_b, 4, 4)
+    ends(w_b, 2, 4)
     begin(1, v_b, left)
     begin(1, v_b, right)
     extend_x(1, v_b)
-    receive(second[:6])
-    ends(w_b, 2, 4)
     first_stage(1, v_b, w_b)
     second_stage(1, v_b, give)
     finish_sends(first + wind_edges + second)
-    for copy in wind_copies:
-        copy.wait_send()
+
+    @pl.loop(0, n_gx - 1)
+    def _(n):
+        wind_arrival(n + (n >= gx).astype(jnp.int32)).wait_send()
 
 
 def solution(mesh):
@@ -358,11 +403,12 @@
                 pltpu.VMEM((2, 2, 8, 8, 128), F32),
                 pltpu.VMEM((4, 128), jnp.int32),
                 pltpu.VMEM((n_gx, 4, 128), F32),
-                pltpu.VMEM((2, 2, 4, 8, 128), F32),
-                pltpu.SemaphoreType.DMA((18,)),
-                pltpu.SemaphoreType.DMA((18,)),
-                pltpu.SemaphoreType.DMA((n_gx - 1,)),
-                pltpu.SemaphoreType.DMA((n_gx - 1,)),
+                pltpu.VMEM((2, 2, 2, 4, 8, 128), F32),
+                pltpu.SemaphoreType.DMA((22,)),
+                pltpu.SemaphoreType.DMA((22,)),
+                pltpu.SemaphoreType.DMA((n_gx,)),
+                pltpu.SemaphoreType.DMA((n_gx,)),
+                pltpu.SemaphoreType.REGULAR((2,)),
                 pltpu.SemaphoreType.DMA((4,)),
             ],
             compiler_params=pltpu.CompilerParams(collective_id=0, has_side_effects=True, vmem_limit_bytes=8 * 1024 * 1024),

time: 23.3 us -> 21.9 us (0.940)
  the two profiles are of different devices: /device:TPU:1 before, /device:TPU:13 now
where the time goes in v3:
time: 21.9 us; the launch traced here: 21.7 us
  Pallas kernels  21.1 us (96%)
  local copies, waits for them, and re-layouts  0.63 us (3%)
    pallas_call x1, Pallas kernels, local(): pl.pallas_call(functools.partial(kernel, n_gx, n_ha), out_shape=jax.Shape...  21.1 us
    unnamed x1, local copies, waits for them, and re-layouts  0.63 us

profile of v3, /device:TPU:13, one launch (start us, length us, event | category | flops | bytes accessed | tf_op | source)
XLA Modules:
  0.0 21.7 jit_solution(2675080635179982192)
XLA Ops:
  0.0 21.1 %reach.1 = f32[4,4,8,128]{3,2,1,0:T(8,128)S(1)} custom-call(f32[4,4,8,128]{3,2,1,0:T(8,128)} %field_hbm.1, s32[2,2,4,128]{3,2,1,0:T(4,128)} %wind_hbm.1, s32[4,128]{1,0:T(4,128)} %obstacle_hbm.1), custom_call_target="tpu_custom_call" | custom-call | tf_op jit(solution)/shard_map/reach/pallas_call | solution.py:387
  21.1 0.6 %copy.5 = f32[4,4,8,128]{3,2,1,0:T(8,128)} copy(f32[4,4,8,128]{3,2,1,0:T(8,128)S(1)} %reach.1) | data formatting | bytes 131072

commit v4 on v3

--- a/solution.py
+++ b/solution.py
@@ -110,23 +110,8 @@
     def _(k):
         signal(barrier, k, ha)
 
-    loads[0].wait()
-    for step in range(STEPS):
-        for part in range(2):
-            own = jnp.abs(wind_int[step, part, 2:6, :].astype(F32) * WIND_SCALE)
-            peaks[gx, pl.ds(2 * step + part, 1), :] = jnp.max(own, axis=0, keepdims=True)
-    rows = lax.broadcasted_iota(jnp.int32, (8, 128), 0)
-    total = 8 * n_ha
-    for tile in range(2):
-        place = rows if tile == 0 else jnp.where(rows < 4, rows + 8, rows - 8)
-        for step in range(STEPS):
-            angle = lax.rem(ha * 8 + place + (total - 4 + 4 * step), total).astype(F32) * head_step
-            for part, value in enumerate((jnp.cos(angle), jnp.sin(angle))):
-                for s in range(4):
-                    drift[step, tile, part, s] = (SPEED_BASE + SPEED_STEP * s) * value
     loads[1].wait()
     loads[2].wait()
-
     pl.semaphore_wait(
         barrier, 1 + gx + has(1).astype(jnp.int32) + has(-1).astype(jnp.int32)
     )
@@ -141,6 +126,7 @@
         low, high = slice(0, 4), slice(4, 8)
         mine, theirs = (high, low) if way > 0 else (low, high)
         inner, outer = (slice(0, 2), slice(6, 8)) if way > 0 else (slice(6, 8), slice(0, 2))
+
         copies, sides = [], ((1, slice(0, 4), slice(6, 8), slice(0, 2)), (-1, slice(8, 12), slice(4, 6), slice(6, 8)))
         for dx, to, near, far in sides:
             near_w = slice(near.start - 2, near.stop - 2)
@@ -154,9 +140,30 @@
             (0, w.at[:, 2:6, theirs], v.at[:, 4:8, theirs], way),
             (0, v.at[:, 4:8, mine], w.at[:, 2:6, mine], way),
         ] + [copies[n] for n in (2, 6, 3, 7)]
-        return [
+        made = [
             (dx, remote(src, dst, base + n, dx, dh)) for n, (dx, src, dst, dh) in enumerate(copies)
         ]
+        relays = [
+            (-1, remote(w.at[:, 2:4, outer], w.at[:, 6:8, outer], base + 1, -1, 0)),
+            (-1, remote(v.at[:, 4:8, theirs], v.at[:, 8:12, theirs], base + 3, -1, 0)),
+        ]
+        return made, relays
+
+    odd = lax.rem(gx, 2) == 1
+
+    def depart(copies):
+        @pl.when(has(-1) & jnp.logical_not(odd))
+        def _():
+            copies[1][1].start()
+            copies[3][1].start()
+
+        start([copies[0], copies[2]] + copies[4:6])
+
+    def relay(copies):
+        @pl.when(odd)
+        def _():
+            for _, copy in copies:
+                copy.start()
 
     def start(copies):
         for dx in (0, 1, -1):
@@ -196,8 +203,8 @@
         else:
             pl.when(has(dx))(run)
 
-    first = halo(v_a, w_a, 0, 1)
-    second = halo(v_b, w_b, 10, -1)
+    first, first_relays = halo(v_a, w_a, 0, 1)
+    second, second_relays = halo(v_b, w_b, 10, -1)
     wind_edges = [
         (1, remote(wind_int.at[:, :, 4:6], wind_int.at[:, :, 0:2], 20, 1, 0)),
         (-1, remote(wind_int.at[:, :, 2:4], wind_int.at[:, :, 6:8], 21, -1, 0)),
@@ -221,8 +228,19 @@
         signal(ready.at[1], k, ha)
 
     upward = [copy for n, copy in enumerate(first) if n in (6, 8)] + wind_edges[:1]
-    start(first[:6])
-    start([copy for n, copy in enumerate(first) if n in (7, 9)] + wind_edges[1:])
+    depart(first)
+    start([copy for n, copy in enumerate(first) if n in (7, 9)])
+
+    loads[0].wait()
+    quarters = lax.broadcasted_iota(jnp.int32, (1, 128), 1) // 32
+    packed = jnp.zeros((1, 128), F32)
+    for step in range(STEPS):
+        for part in range(2):
+            mine = jnp.max(jnp.abs(wind_int[step, part, 2:6, :].astype(F32) * WIND_SCALE), axis=0, keepdims=True)
+            mine = jnp.max(mine, axis=1, keepdims=True)
+            packed = jnp.where(quarters == 2 * step + part, mine, packed)
+    peaks[gx] = packed
+    start(wind_edges[1:])
 
     @pl.loop(0, gx)
     def _(k):
@@ -300,7 +318,8 @@
             swapped = pltpu.roll(limit(candidate, plane), 4, 1)
             v_b[:, 4 + plane, 0:4] = swapped[:, 0:4]
             w_b[:, 2 + plane, 4:8] = swapped[:, 4:8]
-        start(second)
+        depart(second)
+        start(second[6:])
 
     def give(candidate):
         for plane in range(4):
@@ -314,6 +333,16 @@
                     wind_f[step, part, plane] = jnp.broadcast_to(row, (8, 128))
 
     spread(range(2, 6))
+    rows = lax.broadcasted_iota(jnp.int32, (8, 128), 0)
+    total = 8 * n_ha
+    for tile in range(2):
+        place = rows if tile == 0 else jnp.where(rows < 4, rows + 8, rows - 8)
+        for step in range(STEPS):
+            angle = lax.rem(ha * 8 + place + (total - 4 + 4 * step), total).astype(F32) * head_step
+            for part, value in enumerate((jnp.cos(angle), jnp.sin(angle))):
+                for s in range(4):
+                    drift[step, tile, part, s] = (SPEED_BASE + SPEED_STEP * s) * value
+
 
     @pl.when(has(1))
     def _():
@@ -334,6 +363,7 @@
 
     loads[3].wait()
     receive(first[4:6])
+    relay(first_relays)
     begin(0, v_a, own)
     receive(first[:4] + first[6:])
     ends(v_a, 4, 4)
@@ -347,11 +377,12 @@
         wind_arrival(n + (n >= gx).astype(jnp.int32)).wait_recv()
 
     highest = jnp.max(peaks[...], axis=0)
-    highest = jnp.max(highest, axis=1, keepdims=True)
+    quarters = lax.broadcasted_iota(jnp.int32, (1, 128), 1) // 32
+    highest = [jnp.max(jnp.where(quarters == n, highest, 0.0), axis=1, keepdims=True) for n in range(4)]
     alphas, halves = [], []
     for step in range(STEPS):
         pair = [
-            jnp.broadcast_to(SPEED_MAX + highest[2 * step + part : 2 * step + part + 1], (8, 128))
+            jnp.broadcast_to(SPEED_MAX + highest[2 * step + part], (8, 128))
             for part in range(2)
         ]
         alphas.append(pair)
@@ -364,6 +395,7 @@
     second_stage(0, v_a, keep)
 
     receive(second[4:6])
+    relay(second_relays)
     begin(1, v_b, own)
     receive(second[:4] + second[6:])
     ends(v_b, 4, 4)
@@ -402,7 +434,7 @@
                 pltpu.VMEM((2, 2, 8, 128), jnp.int32),
                 pltpu.VMEM((2, 2, 8, 8, 128), F32),
                 pltpu.VMEM((4, 128), jnp.int32),
-                pltpu.VMEM((n_gx, 4, 128), F32),
+                pltpu.VMEM((n_gx, 1, 128), F32),
                 pltpu.VMEM((2, 2, 2, 4, 8, 128), F32),
                 pltpu.SemaphoreType.DMA((22,)),
                 pltpu.SemaphoreType.DMA((22,)),

time: 21.9 us -> 21.3 us (0.973)
  Pallas kernels: 21.1 us -> 20.5 us
    pallas_call x1, Pallas kernels: 21.1 us -> 20.5 us  [local(): pl.pallas_call(functools.partial(kernel, n_gx, n_ha), out_shape=jax.Shape...]
where the time goes in v4:
time: 21.3 us; the launch traced here: 21.1 us
  Pallas kernels  20.5 us (96%)
  local copies, waits for them, and re-layouts  0.63 us (3%)
    pallas_call x1, Pallas kernels, local(): pl.pallas_call(functools.partial(kernel, n_gx, n_ha), out_shape=jax.Shape...  20.5 us
    unnamed x1, local copies, waits for them, and re-layouts  0.63 us

profile of v4, /device:TPU:13, one launch (start us, length us, event | category | flops | bytes accessed | tf_op | source)
XLA Modules:
  0.0 21.1 jit_solution(2643218719621022824)
XLA Ops:
  0.0 20.5 %reach.1 = f32[4,4,8,128]{3,2,1,0:T(8,128)S(1)} custom-call(f32[4,4,8,128]{3,2,1,0:T(8,128)} %field_hbm.1, s32[2,2,4,128]{3,2,1,0:T(4,128)} %wind_hbm.1, s32[4,128]{1,0:T(4,128)} %obstacle_hbm.1), custom_call_target="tpu_custom_call" | custom-call | tf_op jit(solution)/shard_map/reach/pallas_call | solution.py:419
  20.5 0.6 %copy.5 = f32[4,4,8,128]{3,2,1,0:T(8,128)} copy(f32[4,4,8,128]{3,2,1,0:T(8,128)S(1)} %reach.1) | data formatting | bytes 131072

commit v5 on v4

--- a/solution.py
+++ b/solution.py
@@ -221,15 +221,14 @@
             device_id=(k, ha), device_id_type=MESH,
         )
 
+    upward = [copy for n, copy in enumerate(first) if n in (6, 8)] + wind_edges[:1]
+    depart(first)
     pl.when(has(-1))(lambda: signal(ready.at[0], gx - 1, ha))
+    start([copy for n, copy in enumerate(first) if n in (7, 9)])
 
     @pl.loop(0, gx)
     def _(k):
         signal(ready.at[1], k, ha)
-
-    upward = [copy for n, copy in enumerate(first) if n in (6, 8)] + wind_edges[:1]
-    depart(first)
-    start([copy for n, copy in enumerate(first) if n in (7, 9)])
 
     loads[0].wait()
     quarters = lax.broadcasted_iota(jnp.int32, (1, 128), 1) // 32
@@ -248,7 +247,7 @@
 
     half_scale = ACCEL_MAX / SPEED_STEP * 2.0
     head_scale = 2.0 * TURN_RATE / head_step
-    own, left, right = slice(4, 8), slice(2, 4), slice(8, 10)
+    own = slice(4, 8)
 
     def ends(ref, low, count):
         for at_end, edge, next_one, near, far in (
@@ -269,19 +268,18 @@
         velocity = drift[step, tile, 0][:, None] + wind_f[step, 0, planes][None]
         return (back + fore) * velocity, fore - back
 
-    def begin(step, v, planes):
-        place = slice(planes.start - 2, planes.stop - 2)
-        values = v[:, planes]
+    def begin(step, v, plane, count):
+        place = pl.ds(plane - 2, count)
+        values = v[:, pl.ds(plane, count)]
         mean, jump = across(step, 0, place, values)
         known[:, place] = mean - half_scale * speed_terms(values)
         jump_y[:, place] = jump
 
-    def extend_x(step, v):
-        for block in (0, 4):
-            place = slice(block, block + 4)
-            mean, jump = along(step, 0, place, v[:, block : block + 8])
-            known[:, place] = known[:, place] + mean
-            jump_x[:, place] = jump
+    def extend_x(step, v, block):
+        place = pl.ds(block, 4)
+        mean, jump = along(step, 0, place, v[:, pl.ds(block, 8)])
+        known[:, place] = known[:, place] + mean
+        jump_x[:, place] = jump
 
     def whole(step, tile, planes, around, here, other):
         alpha_x, alpha_y = alphas[step]
@@ -292,20 +290,23 @@
             result - head_scale * heading_term(here, other) - half_scale * speed_terms(here)
         )
 
-    def first_stage(step, v, w):
+    def first_stage(step, v, w, block):
         alpha_x, alpha_y = alphas[step]
-        for block in (0, 4):
-            place = slice(block, block + 4)
-            here, other = v[:, block + 2 : block + 6], w[:, place]
-            rest = known[:, place] + alpha_x * jump_x[:, place] + alpha_y * jump_y[:, place]
-            sec_t[:, place] = here + halves[step] * (rest - head_scale * heading_term(here, other))
-        here = w[:, 2:6]
-        sec_w[...] = here + whole(step, 1, slice(2, 6), w[...], here, v[:, own])
+        place = pl.ds(block, 4)
+        here, other = v[:, pl.ds(block + 2, 4)], w[:, place]
+        rest = known[:, place] + alpha_x * jump_x[:, place] + alpha_y * jump_y[:, place]
+        sec_t[:, place] = here + halves[step] * (rest - head_scale * heading_term(here, other))
+
+    def wings(step, v, w, plane, count):
+        planes = pl.ds(plane, count)
+        here, beside = w[:, planes], v[:, pl.ds(plane + 2, count)]
+        change = whole(step, 1, planes, w[:, pl.ds(plane - 2, count + 4)], here, beside)
+        sec_w[:, pl.ds(plane - 2, count)] = here + change
 
     def second_stage(step, v, finish):
         ends(sec_t, 2, 4)
         here = sec_t[:, 2:6]
-        change = whole(step, 0, slice(2, 6), sec_t[...], here, sec_w[...])
+        change = whole(step, 0, pl.ds(2, 4), sec_t[...], here, sec_w[...])
         finish(0.5 * (v[:, own] + (here + change)))
 
     def limit(candidate, plane):
@@ -318,8 +319,8 @@
             swapped = pltpu.roll(limit(candidate, plane), 4, 1)
             v_b[:, 4 + plane, 0:4] = swapped[:, 0:4]
             w_b[:, 2 + plane, 4:8] = swapped[:, 4:8]
+        start(second[6:])
         depart(second)
-        start(second[6:])
 
     def give(candidate):
         for plane in range(4):
@@ -364,17 +365,19 @@
     loads[3].wait()
     receive(first[4:6])
     relay(first_relays)
-    begin(0, v_a, own)
+    begin(0, v_a, 4, 4)
     receive(first[:4] + first[6:])
-    ends(v_a, 4, 4)
-    ends(w_a, 2, 4)
-    begin(0, v_a, left)
-    begin(0, v_a, right)
-    extend_x(0, v_a)
 
     @pl.loop(0, n_gx - 1)
     def _(n):
         wind_arrival(n + (n >= gx).astype(jnp.int32)).wait_recv()
+
+    ends(v_a, 4, 4)
+    ends(w_a, 2, 4)
+    begin(0, v_a, 2, 2)
+    begin(0, v_a, 8, 2)
+    extend_x(0, v_a, 0)
+    extend_x(0, v_a, 4)
 
     highest = jnp.max(peaks[...], axis=0)
     quarters = lax.broadcasted_iota(jnp.int32, (1, 128), 1) // 32
@@ -391,19 +394,36 @@
             / (pair[0] + pair[1] + (TURN_RATE / head_step + ACCEL_MAX / SPEED_STEP))
         )
 
-    first_stage(0, v_a, w_a)
+    first_stage(0, v_a, w_a, 0)
+    first_stage(0, v_a, w_a, 4)
+    wings(0, v_a, w_a, 2, 4)
     second_stage(0, v_a, keep)
 
     receive(second[4:6])
     relay(second_relays)
-    begin(1, v_b, own)
-    receive(second[:4] + second[6:])
+    begin(1, v_b, 4, 4)
+
+    parity = odd.astype(jnp.int32)
+    near, far = 4 - 4 * parity, 4 * parity
+
+    def side(copies, left):
+        for copy in [copy for dx, copy in copies if dx == (1 if left else -1)]:
+            copy.wait_recv()
+
+    pl.when(odd)(functools.partial(side, second, True))
+    pl.when(jnp.logical_not(odd))(functools.partial(side, second, False))
+    begin(1, v_b, 2 + near + near // 2, 2)
+    extend_x(1, v_b, near)
+    first_stage(1, v_b, w_b, near)
+    wings(1, v_b, w_b, 2 + near // 2, 2)
+    pl.when(odd & has(1))(functools.partial(side, second, False))
+    pl.when(jnp.logical_not(odd) & has(-1))(functools.partial(side, second, True))
     ends(v_b, 4, 4)
     ends(w_b, 2, 4)
-    begin(1, v_b, left)
-    begin(1, v_b, right)
-    extend_x(1, v_b)
-    first_stage(1, v_b, w_b)
+    begin(1, v_b, 2 + far + far // 2, 2)
+    extend_x(1, v_b, far)
+    first_stage(1, v_b, w_b, far)
+    wings(1, v_b, w_b, 2 + far // 2, 2)
     second_stage(1, v_b, give)
     finish_sends(first + wind_edges + second)
 

time: 21.3 us -> 20.6 us (0.967)
  Pallas kernels: 20.5 us -> 19.8 us
    pallas_call x1, Pallas kernels: 20.5 us -> 19.8 us  [local(): pl.pallas_call(functools.partial(kernel, n_gx, n_ha), out_shape=jax.Shape...]
where the time goes in v5:
time: 20.6 us; the launch traced here: 20.4 us
  Pallas kernels  19.8 us (96%)
  local copies, waits for them, and re-layouts  0.63 us (3%)
    pallas_call x1, Pallas kernels, local(): pl.pallas_call(functools.partial(kernel, n_gx, n_ha), out_shape=jax.Shape...  19.8 us
    unnamed x1, local copies, waits for them, and re-layouts  0.63 us

profile of v5, /device:TPU:13, one launch (start us, length us, event | category | flops | bytes accessed | tf_op | source)
XLA Modules:
  0.0 20.4 jit_solution(813417015206100793)
XLA Ops:
  0.0 19.8 %reach.1 = f32[4,4,8,128]{3,2,1,0:T(8,128)S(1)} custom-call(f32[4,4,8,128]{3,2,1,0:T(8,128)} %field_hbm.1, s32[2,2,4,128]{3,2,1,0:T(4,128)} %wind_hbm.1, s32[4,128]{1,0:T(4,128)} %obstacle_hbm.1), custom_call_target="tpu_custom_call" | custom-call | tf_op jit(solution)/shard_map/reach/pallas_call | solution.py:439
  19.8 0.6 %copy.5 = f32[4,4,8,128]{3,2,1,0:T(8,128)} copy(f32[4,4,8,128]{3,2,1,0:T(8,128)S(1)} %reach.1) | data formatting | bytes 131072

commit v6 on v5

--- a/solution.py
+++ b/solution.py
@@ -211,15 +211,14 @@
     ]
     def wind_copy(k):
         return pltpu.make_async_remote_copy(
-            src_ref=peaks.at[gx], dst_ref=peaks.at[gx], send_sem=wind_send.at[k], recv_sem=wind_recv.at[gx],
+            src_ref=peaks.at[gx], dst_ref=peaks.at[gx], send_sem=wind_send, recv_sem=wind_recv,
             device_id=(k, ha), device_id_type=MESH,
         )
 
-    def wind_arrival(k):
-        return pltpu.make_async_remote_copy(
-            src_ref=peaks.at[k], dst_ref=peaks.at[k], send_sem=wind_send.at[k], recv_sem=wind_recv.at[k],
-            device_id=(k, ha), device_id_type=MESH,
-        )
+    line = pltpu.make_async_remote_copy(
+        src_ref=peaks.at[0 : n_gx - 1], dst_ref=peaks.at[0 : n_gx - 1], send_sem=wind_send, recv_sem=wind_recv,
+        device_id=(gx, above), device_id_type=MESH,
+    )
 
     upward = [copy for n, copy in enumerate(first) if n in (6, 8)] + wind_edges[:1]
     depart(first)
@@ -249,11 +248,12 @@
     head_scale = 2.0 * TURN_RATE / head_step
     own = slice(4, 8)
 
-    def ends(ref, low, count):
-        for at_end, edge, next_one, near, far in (
+    def ends(ref, low, count, sides=(0, 1)):
+        both = (
             (gx == 0, low, low + 1, low - 1, low - 2),
             (gx == n_gx - 1, low + count - 1, low + count - 2, low + count, low + count + 1),
-        ):
+        )
+        for at_end, edge, next_one, near, far in [both[side] for side in sides]:
             a, b = ref[:, edge], ref[:, next_one]
             ref[:, near] = jnp.where(at_end, 2.0 * a - b, ref[:, near])
             ref[:, far] = jnp.where(at_end, 3.0 * a - 2.0 * b, ref[:, far])
@@ -366,18 +366,8 @@
     receive(first[4:6])
     relay(first_relays)
     begin(0, v_a, 4, 4)
-    receive(first[:4] + first[6:])
-
-    @pl.loop(0, n_gx - 1)
-    def _(n):
-        wind_arrival(n + (n >= gx).astype(jnp.int32)).wait_recv()
-
-    ends(v_a, 4, 4)
-    ends(w_a, 2, 4)
-    begin(0, v_a, 2, 2)
-    begin(0, v_a, 8, 2)
-    extend_x(0, v_a, 0)
-    extend_x(0, v_a, 4)
+    line.wait_recv()
+    receive([pair for pair in first[:4] + first[6:] if pair[0] == 1])
 
     highest = jnp.max(peaks[...], axis=0)
     quarters = lax.broadcasted_iota(jnp.int32, (1, 128), 1) // 32
@@ -394,14 +384,26 @@
             / (pair[0] + pair[1] + (TURN_RATE / head_step + ACCEL_MAX / SPEED_STEP))
         )
 
+    ends(v_a, 4, 4, (0,))
+    ends(w_a, 2, 4, (0,))
+    begin(0, v_a, 2, 2)
+    extend_x(0, v_a, 0)
     first_stage(0, v_a, w_a, 0)
+    wings(0, v_a, w_a, 2, 2)
+    receive([pair for pair in first[:4] + first[6:] if pair[0] == -1])
+    ends(v_a, 4, 4, (1,))
+    ends(w_a, 2, 4, (1,))
+    begin(0, v_a, 8, 2)
+    extend_x(0, v_a, 4)
     first_stage(0, v_a, w_a, 4)
-    wings(0, v_a, w_a, 2, 4)
+    wings(0, v_a, w_a, 4, 2)
     second_stage(0, v_a, keep)
 
     receive(second[4:6])
     relay(second_relays)
     begin(1, v_b, 4, 4)
+    finish_sends(first + wind_edges)
+    line.wait_send()
 
     parity = odd.astype(jnp.int32)
     near, far = 4 - 4 * parity, 4 * parity
@@ -416,6 +418,7 @@
     extend_x(1, v_b, near)
     first_stage(1, v_b, w_b, near)
     wings(1, v_b, w_b, 2 + near // 2, 2)
+    finish_sends(second[6:])
     pl.when(odd & has(1))(functools.partial(side, second, False))
     pl.when(jnp.logical_not(odd) & has(-1))(functools.partial(side, second, True))
     ends(v_b, 4, 4)
@@ -425,11 +428,7 @@
     first_stage(1, v_b, w_b, far)
     wings(1, v_b, w_b, 2 + far // 2, 2)
     second_stage(1, v_b, give)
-    finish_sends(first + wind_edges + second)
-
-    @pl.loop(0, n_gx - 1)
-    def _(n):
-        wind_arrival(n + (n >= gx).astype(jnp.int32)).wait_send()
+    finish_sends(second[:6])
 
 
 def solution(mesh):
@@ -458,8 +457,8 @@
                 pltpu.VMEM((2, 2, 2, 4, 8, 128), F32),
                 pltpu.SemaphoreType.DMA((22,)),
                 pltpu.SemaphoreType.DMA((22,)),
-                pltpu.SemaphoreType.DMA((n_gx,)),
-                pltpu.SemaphoreType.DMA((n_gx,)),
+                pltpu.SemaphoreType.DMA,
+                pltpu.SemaphoreType.DMA,
                 pltpu.SemaphoreType.REGULAR((2,)),
                 pltpu.SemaphoreType.DMA((4,)),
             ],

time: 20.6 us -> 20.1 us (0.976)
  Pallas kernels: 19.8 us -> 19.3 us
    pallas_call x1, Pallas kernels: 19.8 us -> 19.3 us  [local(): pl.pallas_call(functools.partial(kernel, n_gx, n_ha), out_shape=jax.Shape...]
where the time goes in v6:
time: 20.1 us; the launch traced here: 20 us
  Pallas kernels  19.3 us (96%)
  local copies, waits for them, and re-layouts  0.63 us (3%)
    pallas_call x1, Pallas kernels, local(): pl.pallas_call(functools.partial(kernel, n_gx, n_ha), out_shape=jax.Shape...  19.3 us
    unnamed x1, local copies, waits for them, and re-layouts  0.63 us

profile of v6, /device:TPU:13, one launch (start us, length us, event | category | flops | bytes accessed | tf_op | source)
XLA Modules:
  0.0 20.0 jit_solution(7152631425213482780)
XLA Ops:
  0.0 19.3 %reach.1 = f32[4,4,8,128]{3,2,1,0:T(8,128)S(1)} custom-call(f32[4,4,8,128]{3,2,1,0:T(8,128)} %field_hbm.1, s32[2,2,4,128]{3,2,1,0:T(4,128)} %wind_hbm.1, s32[4,128]{1,0:T(4,128)} %obstacle_hbm.1), custom_call_target="tpu_custom_call" | custom-call | tf_op jit(solution)/shard_map/reach/pallas_call | solution.py:438
  19.3 0.6 %copy.5 = f32[4,4,8,128]{3,2,1,0:T(8,128)} copy(f32[4,4,8,128]{3,2,1,0:T(8,128)S(1)} %reach.1) | data formatting | bytes 131072

commit v7 on v6

--- a/solution.py
+++ b/solution.py
@@ -106,14 +106,29 @@
     for dx in (1, -1):
         pl.when(has(dx))(functools.partial(signal, barrier, gx + dx, below))
 
-    @pl.loop(gx + 1, n_gx)
-    def _(k):
-        signal(barrier, k, ha)
+    quarter = n_gx // 4
+
+    def rank(g):
+        four = g // 4
+        moved = (lax.rem(g, 4) == 2) & (four > 0)
+        return jnp.where(moved, n_gx - quarter + four, g - jnp.maximum(g - 3, 0) // 4)
+
+    def column(r):
+        kept = jnp.where(r < 6, r, r + 1 + jnp.maximum(r - 6, 0) // 3)
+        return jnp.where(r > n_gx - quarter, 4 * (r - n_gx + quarter) + 2, kept)
+
+    mine = rank(gx)
+    first_up, first_down = has(1) & (mine > rank(gx + 1)), has(-1) & (mine > rank(gx - 1))
+    later_up, later_down = has(1) & (mine < rank(gx + 1)), has(-1) & (mine < rank(gx - 1))
+
+    @pl.loop(mine + 1, n_gx)
+    def _(r):
+        signal(barrier, column(r), ha)
 
     loads[1].wait()
     loads[2].wait()
     pl.semaphore_wait(
-        barrier, 1 + gx + has(1).astype(jnp.int32) + has(-1).astype(jnp.int32)
+        barrier, 1 + mine + has(1).astype(jnp.int32) + has(-1).astype(jnp.int32)
     )
 
     def remote(src, dst, index, dx, dh):
@@ -220,29 +235,46 @@
         device_id=(gx, above), device_id_type=MESH,
     )
 
-    upward = [copy for n, copy in enumerate(first) if n in (6, 8)] + wind_edges[:1]
+    upward = [copy for n, (_, copy) in enumerate(first) if n in (6, 8)] + [wind_edges[0][1]]
+    downward = [copy for n, (_, copy) in enumerate(first) if n in (7, 9)] + [wind_edges[1][1]]
     depart(first)
-    pl.when(has(-1))(lambda: signal(ready.at[0], gx - 1, ha))
-    start([copy for n, copy in enumerate(first) if n in (7, 9)])
-
-    @pl.loop(0, gx)
-    def _(k):
-        signal(ready.at[1], k, ha)
+
+    @pl.when(first_up)
+    def _():
+        signal(ready.at[0], gx + 1, ha)
+
+    @pl.when(first_down)
+    def _():
+        signal(ready.at[0], gx - 1, ha)
 
     loads[0].wait()
+
+    def begin_x(up, down):
+        for condition, copies in ((up, upward), (down, downward)):
+
+            @pl.when(condition)
+            def _(copies=copies):
+                for copy in copies:
+                    copy.start()
+
+    begin_x(first_up, first_down)
+
+    @pl.loop(0, mine)
+    def _(r):
+        signal(ready.at[1], column(r), ha)
+
     quarters = lax.broadcasted_iota(jnp.int32, (1, 128), 1) // 32
     packed = jnp.zeros((1, 128), F32)
     for step in range(STEPS):
         for part in range(2):
-            mine = jnp.max(jnp.abs(wind_int[step, part, 2:6, :].astype(F32) * WIND_SCALE), axis=0, keepdims=True)
-            mine = jnp.max(mine, axis=1, keepdims=True)
-            packed = jnp.where(quarters == 2 * step + part, mine, packed)
+            largest = jnp.max(jnp.abs(wind_int[step, part, 2:6, :].astype(F32) * WIND_SCALE), axis=0, keepdims=True)
+            largest = jnp.max(largest, axis=1, keepdims=True)
+            packed = jnp.where(quarters == 2 * step + part, largest, packed)
     peaks[gx] = packed
-    start(wind_edges[1:])
-
-    @pl.loop(0, gx)
-    def _(k):
-        wind_copy(k).start()
+
+    @pl.loop(0, mine)
+    def _(r):
+        wind_copy(column(r)).start()
 
     half_scale = ACCEL_MAX / SPEED_STEP * 2.0
     head_scale = 2.0 * TURN_RATE / head_step
@@ -345,19 +377,19 @@
                     drift[step, tile, part, s] = (SPEED_BASE + SPEED_STEP * s) * value
 
 
-    @pl.when(has(1))
+    @pl.when(later_up | later_down)
     def _():
-        pl.semaphore_wait(ready.at[0], 1)
-
-    start(upward)
-
-    @pl.when(gx < n_gx - 1)
+        pl.semaphore_wait(ready.at[0], later_up.astype(jnp.int32) + later_down.astype(jnp.int32))
+
+    begin_x(later_up, later_down)
+
+    @pl.when(mine < n_gx - 1)
     def _():
-        pl.semaphore_wait(ready.at[1], n_gx - 1 - gx)
-
-    @pl.loop(gx + 1, n_gx)
-    def _(k):
-        wind_copy(k).start()
+        pl.semaphore_wait(ready.at[1], n_gx - 1 - mine)
+
+    @pl.loop(mine + 1, n_gx)
+    def _(r):
+        wind_copy(column(r)).start()
 
     receive(wind_edges)
     spread((0, 1, 6, 7))

time: 20.1 us -> 19.6 us (0.975)
  the two profiles are of different devices: /device:TPU:13 before, /device:TPU:123 now
where the time goes in v7:
time: 19.6 us; the launch traced here: 19.5 us
  Pallas kernels  18.8 us (96%)
  local copies, waits for them, and re-layouts  0.63 us (3%)
    pallas_call x1, Pallas kernels, local(): pl.pallas_call(functools.partial(kernel, n_gx, n_ha), out_shape=jax.Shape...  18.8 us
    unnamed x1, local copies, waits for them, and re-layouts  0.63 us

profile of v7, /device:TPU:123, one launch (start us, length us, event | category | flops | bytes accessed | tf_op | source)
XLA Modules:
  0.0 19.5 jit_solution(5720070647583393078)
XLA Ops:
  0.0 18.8 %reach.1 = f32[4,4,8,128]{3,2,1,0:T(8,128)S(1)} custom-call(f32[4,4,8,128]{3,2,1,0:T(8,128)} %field_hbm.1, s32[2,2,4,128]{3,2,1,0:T(4,128)} %wind_hbm.1, s32[4,128]{1,0:T(4,128)} %obstacle_hbm.1), custom_call_target="tpu_custom_call" | custom-call | tf_op jit(solution)/shard_map/reach/pallas_call | solution.py:470
  18.8 0.6 %copy.5 = f32[4,4,8,128]{3,2,1,0:T(8,128)} copy(f32[4,4,8,128]{3,2,1,0:T(8,128)S(1)} %reach.1) | data formatting | bytes 131072

commit v8 on v7

--- a/solution.py
+++ b/solution.py
@@ -395,12 +395,7 @@
     spread((0, 1, 6, 7))
 
     loads[3].wait()
-    receive(first[4:6])
-    relay(first_relays)
-    begin(0, v_a, 4, 4)
     line.wait_recv()
-    receive([pair for pair in first[:4] + first[6:] if pair[0] == 1])
-
     highest = jnp.max(peaks[...], axis=0)
     quarters = lax.broadcasted_iota(jnp.int32, (1, 128), 1) // 32
     highest = [jnp.max(jnp.where(quarters == n, highest, 0.0), axis=1, keepdims=True) for n in range(4)]
@@ -415,6 +410,11 @@
             (0.5 * CFL_NUMBER)
             / (pair[0] + pair[1] + (TURN_RATE / head_step + ACCEL_MAX / SPEED_STEP))
         )
+
+    receive(first[4:6])
+    relay(first_relays)
+    begin(0, v_a, 4, 4)
+    receive([pair for pair in first[:4] + first[6:] if pair[0] == 1])
 
     ends(v_a, 4, 4, (0,))
     ends(w_a, 2, 4, (0,))

time: 19.6 us -> 19.6 us (level)
  the two profiles are of different devices: /device:TPU:123 before, /device:TPU:99 now
where the time goes in v8:
time: 19.6 us; the launch traced here: 19.5 us
  Pallas kernels  18.9 us (96%)
  local copies, waits for them, and re-layouts  0.63 us (3%)
    pallas_call x1, Pallas kernels, local(): pl.pallas_call(functools.partial(kernel, n_gx, n_ha), out_shape=jax.Shape...  18.9 us
    unnamed x1, local copies, waits for them, and re-layouts  0.63 us

profile of v8, /device:TPU:99, one launch (start us, length us, event | category | flops | bytes accessed | tf_op | source)
XLA Modules:
  0.0 19.5 jit_solution(1901996533869988678)
XLA Ops:
  0.0 18.9 %reach.1 = f32[4,4,8,128]{3,2,1,0:T(8,128)S(1)} custom-call(f32[4,4,8,128]{3,2,1,0:T(8,128)} %field_hbm.1, s32[2,2,4,128]{3,2,1,0:T(4,128)} %wind_hbm.1, s32[4,128]{1,0:T(4,128)} %obstacle_hbm.1), custom_call_target="tpu_custom_call" | custom-call | tf_op jit(solution)/shard_map/reach/pallas_call | solution.py:470
  18.9 0.6 %copy.5 = f32[4,4,8,128]{3,2,1,0:T(8,128)} copy(f32[4,4,8,128]{3,2,1,0:T(8,128)S(1)} %reach.1) | data formatting | bytes 131072
